TPU v7x, 128 devices: a whole 4x4x4 slice. The times are simulated.
128 devices in a mesh: seq: 32 (over y_hi, x, z), dp: 4 (over y_lo, core).
Axes of the slice: x: 4, y: 4 (y_hi: 2, y_lo: 2; y = y_hi * 2 + y_lo), z: 4, core: 2. Of those that a mesh axis runs over, the one named last changes fastest.
Arguments:
- teacher_rows: bfloat16 [8192, 8192], P('seq', 'dp'), may hold values from -6 to 6
- teacher_next: bfloat16 [8192, 8192], P('seq', 'dp'), may hold values from -9 to 9
- state_proj: bfloat16 [8192, 256], replicated, may hold values from -0.015625 to 0.015625
- step_proj: bfloat16 [8192, 64], replicated, may hold values from -0.0625 to 0.0625
- rate_log: float32 [64], replicated, may hold values from -12 to 1.2
- step_bias: float32 [64], replicated, may hold values from -1 to 0
- skip_gain: float32 [64], replicated, may hold values from 0.5 to 1.5
Outputs:
- loss_value: float32 [], replicated
- state_proj_grad: float32 [8192, 256], P('dp')
- step_proj_grad: float32 [8192, 64], P('dp')
- rate_log_grad: float32 [64], replicated
- step_bias_grad: float32 [64], replicated
- skip_gain_grad: float32 [64], replicated
All inputs are finite; a program needn't handle non-finite values.
Results may differ from a plain program's by a relative error of at most 0.011.
Values may be sent and summed in bfloat16 or wider, within the bound.
A program may use at most 128 MiB of HBM per device.

v0:
```python
import jax
import jax.numpy as jnp
from jax import lax
from jax.sharding import PartitionSpec as P

BLOCK = 256


def entering_2(value, axis, combine, identity, reverse):
    length, position = (lax.axis_size(axis), lax.axis_index(axis))
    everything = jax.tree.map(lambda part: lax.all_gather(part, axis), value)
    start = jax.tree.map(
        lambda part, zero: jnp.broadcast_to(jnp.asarray(zero, part.dtype), part.shape),
        value,
        identity,
    )

    def lap(k, before):
        at = length - 1 - k if reverse else k
        reached = at > position if reverse else at < position
        new = combine(before, jax.tree.map(lambda part: part[at], everything))
        return jax.tree.map(lambda a, b: jnp.where(reached, a, b), new, before)

    return lax.fori_loop(0, length, lap, start)


def block_terms(bc_block, dt_block, rate_log, step_bias):
    state_width = bc_block.shape[1] // 2
    rounded = bc_block.astype(jnp.bfloat16)
    dt_steps = jax.nn.softplus(dt_block + step_bias)
    log_decay = jnp.cumsum(-jnp.exp(rate_log) * dt_steps, axis=0)
    return (rounded[:, :state_width], rounded[:, state_width:], dt_steps, log_decay)


def block_state(rows_block, b_input, dt_steps, log_decay, head_count):
    block_rows, model_width = rows_block.shape
    decay_total = log_decay[-1]
    weighting = dt_steps * jnp.exp(decay_total - log_decay)
    scaled_rows = (
        (rows_block.reshape(block_rows, head_count, -1) * weighting[:, :, None])
        .reshape(block_rows, model_width)
        .astype(jnp.bfloat16)
    )
    increment = lax.dot_general(
        scaled_rows, b_input, (((0,), (0,)), ((), ())), preferred_element_type=jnp.float32
    )
    return (jnp.exp(decay_total), increment)


def block_output(
    rows_block, b_input, c_output, dt_steps, log_decay, skip_gain, carry_state, head_count
):
    block_rows, model_width = rows_block.shape
    scores = lax.dot_general(
        c_output, b_input, (((1,), (1,)), ((), ())), preferred_element_type=jnp.float32
    )
    row_index = lax.broadcasted_iota(jnp.int32, (block_rows, block_rows), 0)
    col_index = lax.broadcasted_iota(jnp.int32, (block_rows, block_rows), 1)
    causal = (row_index >= col_index)[None]
    log_gap = log_decay.T[:, :, None] - log_decay.T[:, None, :]
    weights = (
        jnp.where(causal, jnp.exp(jnp.where(causal, log_gap, 0.0)), 0.0)
        * scores[None]
        * dt_steps.T[:, None, :]
    )
    weights = weights.astype(jnp.bfloat16)
    inputs = rows_block.reshape(block_rows, head_count, -1)
    inner_term = jnp.einsum("hts,shp->thp", weights, inputs, preferred_element_type=jnp.float32)
    carried = lax.dot_general(
        c_output.astype(jnp.float32),
        carry_state,
        (((1,), (1,)), ((), ())),
        precision=lax.Precision.HIGHEST,
    )
    output = (
        inner_term
        + carried.reshape(inner_term.shape) * jnp.exp(log_decay)[:, :, None]
        + skip_gain[None, :, None] * inputs
    )
    return output.reshape(block_rows, model_width)


def spread(decays, carry_state):
    return jnp.repeat(decays, carry_state.shape[0] // decays.shape[0])[:, None] * carry_state


def combine(earlier, later):
    return (earlier[0] * later[0], spread(later[0], earlier[1]) + later[1])


def chain_states(decays, increments, start_state):

    def advance(carry, block_items):
        carry_state, decay_total = carry
        return (
            (spread(block_items[0], carry_state) + block_items[1], decay_total * block_items[0]),
            carry_state,
        )

    (end_state, decay_total), incoming = lax.scan(
        advance, (start_state, jnp.ones_like(decays[0])), (decays, increments)
    )
    return (incoming, end_state, decay_total)


def shards(teacher_rows, teacher_next, state_proj, step_proj, rate_log, step_bias, skip_gain):
    seq_rows, local_width = teacher_rows.shape
    dp_count = lax.axis_size("dp")
    member = lax.axis_index("dp")
    head_count = rate_log.shape[0]
    local_heads = head_count // dp_count
    state_width = state_proj.shape[1] // 2
    block_rows = min(BLOCK, seq_rows)
    block_count = seq_rows // block_rows
    tokens_all = seq_rows * lax.axis_size("seq")
    joined = jnp.concatenate([state_proj, step_proj], axis=1)
    proj_all = jnp.dot(
        lax.all_gather(teacher_rows, "dp", axis=1, tiled=True),
        joined,
        preferred_element_type=jnp.float32,
    )
    proj_bc = proj_all[:, : 2 * state_width]
    proj_dt = proj_all[:, 2 * state_width :]
    head_start = member * local_heads
    own_dt = lax.dynamic_slice_in_dim(proj_dt, head_start, local_heads, 1)
    own_rate = lax.dynamic_slice_in_dim(rate_log, head_start, local_heads, 0)
    own_bias = lax.dynamic_slice_in_dim(step_bias, head_start, local_heads, 0)
    own_skip = lax.dynamic_slice_in_dim(skip_gain, head_start, local_heads, 0)
    pieces_rows = teacher_rows.reshape(block_count, block_rows, local_width)
    pieces_target = teacher_next.reshape(block_count, block_rows, local_width)

    def summaries(proj_bc, own_dt, own_rate, own_bias):

        def summaries_per_block(block_items):
            rows_block, bc_block, dt_block = block_items
            b_input, c_output, dt_steps, log_decay = block_terms(
                bc_block, dt_block, own_rate, own_bias
            )
            return block_state(rows_block, b_input, dt_steps, log_decay, local_heads)

        return lax.map(
            summaries_per_block,
            (
                pieces_rows,
                proj_bc.reshape(block_count, block_rows, -1),
                own_dt.reshape(block_count, block_rows, local_heads),
            ),
        )

    def local_end(decays, increments):
        _, end_state, decay_total = chain_states(
            decays, increments, jnp.zeros((local_width, state_width), jnp.float32)
        )
        return (end_state, decay_total)

    def entering(decays, increments, start_state):
        return chain_states(decays, increments, start_state)[0]

    def errors(proj_bc, own_dt, own_rate, own_bias, own_skip, incoming):

        def errors_per_block(block_items):
            rows_block, target_block, bc_block, dt_block, carry_state = block_items
            b_input, c_output, dt_steps, log_decay = block_terms(
                bc_block, dt_block, own_rate, own_bias
            )
            output = block_output(
                rows_block,
                b_input,
                c_output,
                dt_steps,
                log_decay,
                own_skip,
                carry_state,
                local_heads,
            )
            residual = output - target_block.astype(jnp.float32)
            return jnp.sum(residual * residual)

        block_sums = lax.map(
            errors_per_block,
            (
                pieces_rows,
                pieces_target,
                proj_bc.reshape(block_count, block_rows, -1),
                own_dt.reshape(block_count, block_rows, local_heads),
                incoming,
            ),
        )
        return jnp.sum(block_sums) / (2.0 * tokens_all)

    (decays, increments), pull_summary = jax.vjp(summaries, proj_bc, own_dt, own_rate, own_bias)
    (end_state, decay_total), pull_end = jax.vjp(local_end, decays, increments)
    identity = (jnp.ones_like(decay_total), jnp.zeros_like(end_state))
    _, state_before = entering_2((decay_total, end_state), "seq", combine, identity, False)
    incoming, pull_entering = jax.vjp(entering, decays, increments, state_before)
    partial_loss, pull_errors = jax.vjp(
        errors, proj_bc, own_dt, own_rate, own_bias, own_skip, incoming
    )
    err_grad_bc, err_grad_dt, err_grad_rate, err_grad_bias, err_grad_skip, grad_incoming = (
        pull_errors(jnp.ones((), jnp.float32))
    )
    in_grad_decays, in_grad_increments, grad_before = pull_entering(grad_incoming)
    _, grad_after = entering_2((decay_total, grad_before), "seq", combine, identity, True)
    grad_decay_total = jnp.sum((grad_after * state_before).reshape(local_heads, -1), axis=1)
    end_grad_decays, end_grad_increments = pull_end((grad_after, grad_decay_total))
    sum_grad_bc, sum_grad_dt, sum_grad_rate, sum_grad_bias = pull_summary(
        (in_grad_decays + end_grad_decays, in_grad_increments + end_grad_increments)
    )
    grad_dt_cols = lax.dynamic_update_slice_in_dim(
        jnp.zeros((seq_rows, head_count), jnp.float32), err_grad_dt + sum_grad_dt, head_start, 1
    )
    head_partial = jnp.concatenate([err_grad_bc + sum_grad_bc, grad_dt_cols], axis=1)
    proj_grads = lax.psum(head_partial, "dp").astype(jnp.bfloat16)
    weight_part = lax.dot_general(
        teacher_rows, proj_grads, (((0,), (0,)), ((), ())), preferred_element_type=jnp.float32
    )
    summed = lax.psum(weight_part, "seq")
    empty_heads = jnp.zeros((head_count,), jnp.float32)
    rate_part = lax.dynamic_update_slice_in_dim(
        empty_heads, err_grad_rate + sum_grad_rate, head_start, 0
    )
    bias_part = lax.dynamic_update_slice_in_dim(
        empty_heads, err_grad_bias + sum_grad_bias, head_start, 0
    )
    skip_part = lax.dynamic_update_slice_in_dim(empty_heads, err_grad_skip, head_start, 0)
    loss_total, total_rate, total_bias, total_skip = lax.psum(
        (partial_loss, rate_part, bias_part, skip_part), ("seq", "dp")
    )
    model_width = local_width * dp_count
    return (
        loss_total / model_width,
        summed[:, : 2 * state_width],
        summed[:, 2 * state_width :],
        total_rate,
        total_bias,
        total_skip,
    )


def solution(mesh):
    placed = (P("seq", "dp"), P("seq", "dp"), P(), P(), P(), P(), P())
    return jax.shard_map(
        shards,
        mesh=mesh,
        in_specs=placed,
        out_specs=(P(), P("dp", None), P("dp", None), P(), P(), P()),
        check_vma=False,
    )
```

profile of v0, /device:TPU:0, one launch (start us, length us, event | category | flops | bytes accessed | tf_op | source)
XLA Modules:
  0.0 1166.7 jit_solution(7682827022488553899)
XLA Ops:
  8.0 2.0 copy.75
  10.2 48.0 %all-gather.7.cloned.1.call-done = bf16[256,8192]{1,0:T(8,128)(2,1)} async-done(((bf16[256,2048]{1,0:T(8,128)(2,1)}), bf16[256,8192]{1,0:T(8,128)(2,1)}) %all-gather.7.cloned.1.call-update) | async-done | bytes 4194320 | tf_op jit(solution)/shard_map/all_gather | solution.py:118
  58.2 5.3 fusion.71
  68.6 2.1 convolution_add_fusion.1
  74.4 95.3 %all-gather.2 = f32[32,1,16]{2,1,0:T(1,128)} all-gather(f32[1,1,16]{2,1,0:T(1,128)S(1)} %bitcast.226), channel_id=1, replica_groups=mesh['seq'=32,'dp'=4] {'seq'}, dimensions={0}, use_global_device_ids=true | all-gather | bytes 2112 | tf_op jit(solution)/shard_map/all_gather | solution.py:11
  170.7 160.9 %all-gather.9.cloned.1.call-done = f32[65536,128]{1,0:T(8,128)} async-done(((f32[2048,128]{1,0:T(8,128)}), f32[65536,128]{1,0:T(8,128)}) %all-gather.9.cloned.1.call-update) | async-done | bytes 33554448 | tf_op jit(solution)/shard_map/all_gather | solution.py:11
  331.6 81.9 %while.25 = (s32[]{:T(128)}, f32[2048,128]{1,0:T(8,128)S(1)}, s32[]{:T(128)}, f32[32,16]{1,0:T(8,128)}, f32[32,2048,128]{2,1,0:T(8,128)}, /*index=5*/s32[]{:T(128)}, s32[]{:T(128)}) while((s32[]{:T(128)}, f32[2048,128]{1,0:T(8,128)S(1)}, s32[]{:T(128)}, f32[32,16]{1,0:T(8,128)}, f32[32,2048,128]{2,1,0:T(8,128)}, ...), condition=%wide.region_3.5_spmd.clone, body=%wide.region_2.4_spmd.clone.sunk | while | flops 1048580 | bytes 3162409 | solution.py:24
  332.3 1.8 fusion.87
  334.9 1.8 fusion.87
  337.5 1.8 fusion.87
  340.0 1.8 fusion.87
  342.6 1.8 fusion.87
  345.1 1.8 fusion.87
  347.7 1.8 fusion.87
  350.3 1.8 fusion.87
  352.8 1.8 fusion.87
  355.4 1.8 fusion.87
  358.0 1.8 fusion.87
  360.5 1.8 fusion.87
  368.2 1.8 fusion.87
  370.8 1.8 fusion.87
  375.9 1.8 fusion.87
  381.0 1.8 fusion.87
  386.1 1.8 fusion.87
  391.2 1.8 fusion.87
  393.8 1.8 fusion.87
  396.4 1.8 fusion.87
  415.4 4.6 multiply_reduce_fusion.1
  420.1 2.9 copy.82
  424.9 3.4 convolution_add_fusion
  428.6 4.3 fusion.20
  432.9 2.9 copy.84
  435.8 3.2 multiply_reduce_fusion
  439.8 3.9 fusion.16
  443.9 2.5 reduce-window.48
  447.3 5.2 convolution_convert_fusion.2
  452.7 232.9 %all-gather.11.cloned.1.call-done = f32[65536,128]{1,0:T(8,128)} async-done(((f32[2048,128]{1,0:T(8,128)}), f32[65536,128]{1,0:T(8,128)}) %all-gather.11.cloned.1.call-update) | async-done | bytes 33554448 | tf_op jit(solution)/shard_map/all_gather | solution.py:11
  685.5 82.2 %while.26 = (s32[]{:T(128)}, f32[2048,128]{1,0:T(8,128)S(1)}, s32[]{:T(128)}, f32[32,16]{1,0:T(8,128)}, f32[32,2048,128]{2,1,0:T(8,128)}, /*index=5*/s32[]{:T(128)}, s32[]{:T(128)}, s32[]{:T(128)}, s32[]{:T(128)}) while((s32[]{:T(128)}, f32[2048,128]{1,0:T(8,128)S(1)}, s32[]{:T(128)}, f32[32,16]{1,0:T(8,128)}, ...), condition=%wide.region_8.10_spmd.clone, body=%wide.region_7.9_spmd.clone.sunk | while | flops 1048584 | bytes 3162471 | solution.py:24
  767.7 2.4 convolution_convert_fusion.3
  771.0 1.8 fusion.17
  773.1 1.9 copy.89
  777.1 2.5 reduce-window.50
  780.1 14.3 %all-reduce.9 = bf16[256,320]{0,1:T(8,128)(2,1)S(1)} all-reduce(f32[256,320]{0,1:T(8,128)S(1)} %pad_maximum_fusion), channel_id=1, replica_groups=mesh['seq'=32,'dp'=4] {'dp'}, use_global_device_ids=true, to_apply=%region_25.27 | all-reduce | flops 81920 | bytes 491520 | tf_op jit(solution)/shard_map/psum | solution.py:213
  794.4 2.0 convolution_bitcast_fusion
  798.6 65.1 %all-reduce.4 = (f32[]{:T(128)}, f32[64]{0:T(128)}, f32[64]{0:T(128)}, f32[64]{0:T(128)}) all-reduce(f32[]{:T(128)S(6)} %div.6, f32[64]{0:T(128)S(1)} %multiply_dynamic-update-slice_fusion, f32[64]{0:T(128)S(1)} %add_dynamic-update-slice_fusion.1, f32[64]{0:T(128)S(1)} %dynamic_update_slice.109), channel_id=1, replica_groups=mesh['seq'=32,'dp'=4] {'seq','dp'}, use_global_device_ids=true, to_apply=%region_5.7 | all-reduce | flops 193 | bytes 1544 | tf_op jit(solution)/shard_map/psum | solution.py:226
  864.4 289.4 %all-reduce.8.cloned.1.call-done = f32[2048,320]{0,1:T(8,128)} async-done(((f32[2048,320]{0,1:T(8,128)}), f32[2048,320]{0,1:T(8,128)}) %all-reduce.8.cloned.1.call-update) | async-done | bytes 2621456 | tf_op jit(solution)/shard_map/psum | solution.py:217
  1155.4 1.8 copy.94
  1157.2 1.9 slice.93
  (312 shorter events, 150.2 us)
Async XLA Ops:
  7.2 2.8 copy-start.34
  7.2 2.9 copy-start.32
  7.2 51.0 %all-gather.7.cloned.1.call-start = ((), (), s32[]{:S(2)}) async-start(), calls=%async_computation | async-start | bytes 5242880 | tf_op jit(solution)/shard_map/all_gather | solution.py:118
  7.9 323.6 %all-gather.9.cloned.1.call-start = ((), (), s32[]{:S(2)}) async-start(), calls=%async_computation.2 | async-start | bytes 34603008 | tf_op jit(solution)/shard_map/all_gather | solution.py:11
  10.1 55.7 %copy-start.25 = (f32[16]{0:T(128)}, f32[16]{0:T(128)S(1)}, u32[]{:S(2)}) copy-start(f32[16]{0:T(128)S(1)} %dynamic_slice.156) | copy-start | bytes 196
  10.2 53.3 %copy-start.29 = (f32[16]{0:T(128)}, f32[16]{0:T(128)S(1)}, u32[]{:S(2)}) copy-start(f32[16]{0:T(128)S(1)} %fusion.61) | copy-start | bytes 196
  63.5 5.1 copy-start
  63.5 3.0 copy-start.11
  64.4 6.3 copy-start.16
  65.1 1.4 copy-start.14
  65.8 4.9 copy-start.27
  67.3 1.3 copy-start.3
  70.7 1.4 copy-start.35
  70.7 2.0 copy-start.4
  70.7 614.8 %all-gather.11.cloned.1.call-start = ((), (), s32[]{:S(2)}) async-start(), calls=%async_computation.3 | async-start | bytes 34603008 | tf_op jit(solution)/shard_map/all_gather | solution.py:11
  72.1 2.3 copy-start.31
  413.5 1.2 copy-start.7
  413.5 1.9 copy-start.9
  413.5 1.9 copy-start.21
  413.5 1.9 copy-start.22
  413.5 1.9 copy-start.24
  413.5 1.9 copy-start.36
  414.6 5.5 copy-start.5
  423.0 1.9 copy-start.1
  423.6 1.3 copy-start.2
  428.4 725.4 %all-reduce.8.cloned.1.call-start = ((), (), s32[]{:S(2)}) async-start(), calls=%async_computation.1 | async-start | bytes 5242880 | tf_op jit(solution)/shard_map/psum | solution.py:217
  435.8 3.6 copy-start.6
  435.8 4.0 copy-start.8
  435.8 4.0 copy-start.10
  435.8 4.0 copy-start.23
  439.8 3.9 copy-start.17
  775.0 1.6 copy-start.12
  775.1 1.6 copy-start.18
  775.1 1.6 copy-start.26
  775.1 1.6 copy-start.28
  775.1 1.9 copy-start.15
  775.1 4.7 copy-start.13
  775.1 4.7 copy-start.20
  775.1 4.7 copy-start.30
  796.4 0.7 copy-start.19
  796.4 2.0 copy-start.33
  1153.8 1.6 slice-start
Sparse Core Ops, SparseCore 0:
  9.7 48.4 all-gather.6
  70.9 260.6 all-gather.8
  428.5 256.9 all-gather.10
  796.6 357.2 all-reduce.7
where the time goes:
time: 1170 us
  waiting for transfers between devices  732 us (63%)
  blocking collectives  175 us (15%)
  other arithmetic  133 us (11%)
  local copies, waits for them, and re-layouts  74.6 us (6%)
  matrix products  33.7 us (3%)
  between operations  16.7 us (1%)
    all_gather x2, waiting for transfers between devices, entering_2(): everything = jax.tree.map(lambda part: lax.all_gather(part, axis), value)  394 us
    psum x1, waiting for transfers between devices, shards(): summed = lax.psum(weight_part, 'seq')  289 us
    select_n x64, other arithmetic, lap(): return jax.tree.map(lambda a, b: jnp.where(reached, a, b), new, before)  114 us
    all_gather x1, blocking collectives, entering_2(): everything = jax.tree.map(lambda part: lax.all_gather(part, axis), value)  95.3 us
    psum x1, blocking collectives, shards(): lax.psum((partial_loss, rate_part, bias_part, skip_part), ('seq', 'dp'))  65.1 us
    all_gather x1, waiting for transfers between devices, shards(): lax.all_gather(teacher_rows, 'dp', axis=1, tiled=True)  48 us
    squeeze x64, local copies, waits for them, and re-layouts, lap(): new = combine(before, jax.tree.map(lambda part: part[at], everything))  44 us
  transfers between devices with their start and end apart: 4, of which 4 were waited for; matrix products, arithmetic and copies ran while one was open for 3% of the time, Pallas kernels for 0%

commit v1 on v0

v1 whole, which is shorter than its diff:
```python
import functools

import jax
import jax.numpy as jnp
from jax import lax
from jax.experimental import pallas as pl
from jax.experimental.pallas import tpu as pltpu
from jax.sharding import PartitionSpec as P

SEQ, DP = 32, 4
T = 256
WIDTH = 2048
HEADS = 64
PAIRS = 8
N = 128
PIECE = 64
MESH = pl.DeviceIdType.MESH
BF, F32 = jnp.bfloat16, jnp.float32
SCALE = 1.0 / 8192.0


def dot(a, b):
    return jnp.dot(a, b, preferred_element_type=F32)


def dot_nt(a, b):
    return lax.dot_general(a, b, (((1,), (1,)), ((), ())), preferred_element_type=F32)


def split3(v):
    hi = v.astype(BF).astype(F32)
    rest = v - hi
    mid = rest.astype(BF).astype(F32)
    return hi, mid, rest - mid


def tri_sum(tri, v):
    return sum(dot(tri, part.astype(BF)) for part in split3(v))


def send(src, dst, send_sem, recv_sem, device):
    pltpu.make_async_remote_copy(
        src_ref=src, dst_ref=dst, send_sem=send_sem, recv_sem=recv_sem,
        device_id=device, device_id_type=MESH,
    ).start()


def wait_for(ref, sem):
    pltpu.make_async_copy(ref, ref, sem).wait()


def loop(count, body):
    lax.fori_loop(0, count, lambda k, c: (body(k), c)[1], 0)


def pack_rows(v):
    return jnp.concatenate([v[:32], v[32:]], axis=1)


def unpack_rows(ref):
    parts = []
    for q in range(DP):
        parts += [ref[q][:, :64], ref[q][:, 64:]]
    return jnp.concatenate(parts, axis=0)


def kernel(
    x_ref, tgt_ref, sp_ref, st_ref, rate_ref, bias_ref, skip_ref,
    out_ref, small_ref,
    w_bc, w_dt, xt_ref,
    p_bc, p_dt, r_bc, r_dt, f_bc, f_dt,
    p2_bc, p2_dt, r2_bc, r2_dt, f2_bc, f2_dt,
    stack_ref, rows_ref, cx_ref, sk_ref, sc_ref, xdt_ref, l_ref, z_ref, err_ref, de_ref,
    sm_ref, dsc_ref, dc_ref, db_ref, k_ref, a_ref, dw_ref, acc_ref,
    es_ref, re_ref, sf_ref, rs_ref, gs_ref, rg_ref, sh_ref, rh_ref, dec_ref,
    ws_ref, rw_ref, sums_ref, sroot_ref, sdp_ref, sfin_ref,
    ssem, rsem, lsem,
):
    me, dq = lax.axis_index("seq"), lax.axis_index("dp")
    head0 = dq * (HEADS // DP)

    def peer(k):
        return lax.rem(me + k, SEQ)

    def member(k):
        return lax.rem(dq + k, DP)

    barrier = pltpu.get_barrier_semaphore()
    loop(SEQ - 1, lambda k: pl.semaphore_signal(
        barrier, inc=1, device_id=(peer(k + 1), dq), device_id_type=MESH))
    loop(DP - 1, lambda k: pl.semaphore_signal(
        barrier, inc=1, device_id=(me, member(k + 1)), device_id_type=MESH))

    own = pl.ds(pl.multiple_of(dq * WIDTH, WIDTH), WIDTH)
    load_bc = pltpu.make_async_copy(sp_ref.at[own], w_bc, lsem.at[0])
    load_dt = pltpu.make_async_copy(st_ref.at[own], w_dt, lsem.at[1])
    load_bc.start()
    load_dt.start()
    load_bc.wait()
    load_dt.wait()

    def dp_sum(bc, dt, p_bc, p_dt, r_bc, r_dt, f_bc, f_dt, sem):
        for q in range(DP):
            p_bc[q] = bc[64 * q : 64 * q + 64].astype(BF)
            p_dt[q] = pack_rows(dt[64 * q : 64 * q + 64])
        if sem == 0:
            pl.semaphore_wait(barrier, SEQ + DP - 2)
        for k in range(1, DP):
            q = member(k)
            send(p_bc.at[q], r_bc.at[dq], ssem.at[sem], rsem.at[sem], (me, q))
            send(p_dt.at[q], r_dt.at[dq], ssem.at[sem + 1], rsem.at[sem + 1], (me, q))
        r_bc[dq] = p_bc[dq]
        r_dt[dq] = p_dt[dq]
        wait_for(r_bc.at[pl.ds(0, DP - 1)], rsem.at[sem])
        wait_for(r_dt.at[pl.ds(0, DP - 1)], rsem.at[sem + 1])
        f_bc[dq] = sum(r_bc[q].astype(F32) for q in range(DP)).astype(BF)
        f_dt[dq] = sum(r_dt[q] for q in range(DP))
        for k in range(1, DP):
            q = member(k)
            send(f_bc.at[dq], f_bc.at[dq], ssem.at[sem + 2], rsem.at[sem + 2], (me, q))
            send(f_dt.at[dq], f_dt.at[dq], ssem.at[sem + 3], rsem.at[sem + 3], (me, q))
        wait_for(f_bc.at[pl.ds(0, DP - 1)], rsem.at[sem + 2])
        wait_for(f_dt.at[pl.ds(0, DP - 1)], rsem.at[sem + 3])

    x_all = x_ref[...]
    dp_sum(dot(x_all, w_bc[...]), dot(x_all, w_dt[...]),
           p_bc, p_dt, r_bc, r_dt, f_bc, f_dt, 0)

    bc = f_bc[...].reshape(T, 2 * N)
    b_in, c_out = bc[:, :N], bc[:, N:]
    b_t = b_in.astype(F32).T.astype(BF)
    c_t = c_out.astype(F32).T.astype(BF)
    pre = unpack_rows(f_dt) + bias_ref[...]
    dt = jnp.maximum(pre, 0.0) + jnp.log1p(jnp.exp(-jnp.abs(pre)))
    rate = jnp.exp(rate_ref[...])
    log_rate = -rate * dt
    row_i = lax.broadcasted_iota(jnp.int32, (T, T), 0)
    col_i = lax.broadcasted_iota(jnp.int32, (T, T), 1)
    tri = jnp.where(row_i >= col_i, 1.0, 0.0).astype(BF)
    cum = tri_sum(tri, log_rate)
    cend = cum[T - 1 : T]
    rows_ref[...] = jnp.concatenate([cum, dt], axis=1).T
    skip8 = jnp.broadcast_to(skip_ref[...], (16, HEADS))
    for at, v in ((0, cum), (T, dt), (2 * T, skip8)):
        stack_ref[at : at + v.shape[0]] = jnp.concatenate(split3(v), axis=1).astype(BF)
    sel_row = lax.rem(lax.broadcasted_iota(jnp.int32, (3 * HEADS, 2 * N), 0), HEADS)
    sel_col = lax.broadcasted_iota(jnp.int32, (3 * HEADS, 2 * N), 1) // N

    def cols(hp):
        return pl.ds(pl.multiple_of(hp * 2 * N, 2 * N), 2 * N)

    def start_pair(k):
        return lax.rem(me // 4 + k, PAIRS)

    def send_pair(hp, src, dst, sem):
        for i in range(4):
            o = 4 * hp + i

            @pl.when(o != me)
            def _():
                send(src.at[o], dst.at[me], ssem.at[sem], rsem.at[sem], (o, dq))

    def put_pair(ref, hp, value):
        for i in range(4):
            half, j = i % 2, i // 2
            ref[4 * hp + i, 0:PIECE] = value[
                half * PIECE : (half + 1) * PIECE, j * N : (j + 1) * N].astype(BF)

    def get_pair(ref, hp):
        v = ref[pl.ds(4 * hp, 4)]
        return jnp.concatenate([v[:2].reshape(N, N), v[2:].reshape(N, N)], axis=1)

    def increments(k):
        hp = start_pair(k)
        sel = jnp.where(sel_row == head0 + 2 * hp + sel_col, 1.0, 0.0).astype(BF)
        wide = dot(stack_ref[...], sel)
        cx, dx = wide[:T], wide[T : 2 * T]
        cx_ref[hp] = cx
        sk_ref[hp] = wide[2 * T : 2 * T + 8]
        xp = x_ref[:, cols(hp)].astype(F32)
        xd = xp * dx
        xdt_ref[hp] = xd.astype(BF)
        last = cx[T - 1 : T]
        sc = (xd * jnp.exp(last - cx)).astype(BF)
        sc_ref[hp] = sc
        put_pair(es_ref, hp, dot(b_t, sc))
        hi = last.astype(BF).astype(F32)
        both = jnp.concatenate(
            [jnp.broadcast_to(hi, (8, 2 * N)), jnp.broadcast_to(last - hi, (8, 2 * N))], axis=0
        ).astype(BF)
        for i in range(4):
            es_ref[4 * hp + i, PIECE : PIECE + 16] = both[:, (i // 2) * N : (i // 2 + 1) * N]
        send_pair(hp, es_ref, re_ref, 4)

    loop(PAIRS, increments)
    re_ref[me] = es_ref[me]

    sm_ref[...] = jnp.where(row_i >= col_i, dot_nt(c_out, b_in), 0.0)

    def in_block(hp):
        parts = []
        for j in range(2):
            cx = cx_ref[hp, :, j * N : (j + 1) * N]
            gap = jnp.concatenate([cx, cx], axis=1) - rows_ref[pl.ds(head0 + 2 * hp + j, 1), :]
            decay = jnp.exp(jnp.minimum(gap, 0.0))
            l_ref[2 * hp + j] = decay.astype(BF)
            w = (decay * sm_ref[...]).astype(BF)
            parts.append(dot(w, xdt_ref[hp, :, j * N : (j + 1) * N]))
        z_ref[hp] = jnp.concatenate(parts, axis=1)

    loop(PAIRS, in_block)

    wait_for(re_ref.at[pl.ds(0, SEQ - 1)], rsem.at[4])

    def forward(j, state):
        sf_ref[j] = state.reshape(PIECE, N).astype(BF)
        tail = re_ref[j, PIECE : PIECE + 16].astype(F32)
        decay = jnp.exp(tail[:8] + tail[8:])
        dec_ref[j] = decay
        return decay[None] * state + re_ref[j, 0:PIECE].astype(F32).reshape(8, 8, N)

    lax.fori_loop(0, SEQ, forward, jnp.zeros((8, 8, N), F32))
    loop(SEQ - 1, lambda k: send(
        sf_ref.at[peer(k + 1)], rs_ref.at[me], ssem.at[5], rsem.at[5], (peer(k + 1), dq)))
    rs_ref[me] = sf_ref[me]

    def turn(i):
        at = pl.ds(pl.multiple_of(i * 2 * N, 2 * N), 2 * N)
        xt_ref[at, :] = x_ref[:, at].astype(F32).T.astype(BF)

    loop(PAIRS, turn)
    acc_ref[...] = jnp.zeros_like(acc_ref)
    wait_for(rs_ref.at[pl.ds(0, SEQ - 1)], rsem.at[5])

    def errors(k):
        hp = start_pair(k)
        at = cols(hp)
        decay = jnp.exp(cx_ref[hp])
        z = z_ref[hp] + dot(c_out, get_pair(rs_ref, hp)) * decay
        z_ref[hp] = z
        err = (z + sk_ref[hp][:1] * x_ref[:, at].astype(F32)) - tgt_ref[:, at].astype(F32)
        err_ref[hp] = err
        de = (err * decay).astype(BF)
        de_ref[hp] = de
        put_pair(gs_ref, hp, dot(c_t, de))
        send_pair(hp, gs_ref, rg_ref, 6)
        acc_ref[0:8] += jnp.sum((err * err).reshape(T // 8, 8, 2 * N), axis=0)

    loop(PAIRS, errors)
    rg_ref[me] = gs_ref[me]

    lane = lax.broadcasted_iota(jnp.int32, (T, HEADS), 1)
    lane1 = lax.broadcasted_iota(jnp.int32, (1, HEADS), 1)
    for ref in (dsc_ref, dc_ref, db_ref, k_ref, a_ref, dw_ref):
        ref[...] = jnp.zeros_like(ref)
    acc_ref[8:16] = jnp.zeros((8, 2 * N), F32)

    def grads_in_block(hp):
        at = cols(hp)
        xp = x_ref[:, at]
        err = err_ref[hp]
        errb = err.astype(BF)
        dc_ref[...] += dot_nt(de_ref[hp], get_pair(rs_ref, hp))
        rowed = err * z_ref[hp]
        skipped = jnp.sum(err * xp.astype(F32), axis=0, keepdims=True)
        for j in range(2):
            head = head0 + 2 * hp + j
            sub = slice(j * N, (j + 1) * N)
            dwd = dot_nt(errb[:, sub], xp[:, sub]) * l_ref[2 * hp + j].astype(F32)
            dsc_ref[...] += dwd * rows_ref[pl.ds(HEADS + head, 1), :]
            k_ref[pl.ds(head, 1), :] = jnp.sum(dwd * sm_ref[...], axis=0, keepdims=True)
            a_ref[...] += jnp.where(
                lane == head, jnp.sum(rowed[:, sub], axis=1, keepdims=True), 0.0)
            acc_ref[8:9, :HEADS] += jnp.where(
                lane1 == head, jnp.sum(skipped[:, sub], axis=1, keepdims=True), 0.0)

    loop(PAIRS, grads_in_block)
    dsc = jnp.where(row_i >= col_i, dsc_ref[...], 0.0)
    dc_ref[...] += dot(dsc.astype(BF), b_in)
    db_ref[...] += dot(dsc.T.astype(BF), c_out)

    wait_for(rg_ref.at[pl.ds(0, SEQ - 1)], rsem.at[6])

    def backward(i, state):
        j = SEQ - 1 - i
        sh_ref[j] = state.reshape(PIECE, N).astype(BF)
        return dec_ref[j][None] * state + rg_ref[j].astype(F32).reshape(8, 8, N)

    lax.fori_loop(0, SEQ, backward, jnp.zeros((8, 8, N), F32))
    loop(SEQ - 1, lambda k: send(
        sh_ref.at[peer(k + 1)], rh_ref.at[me], ssem.at[7], rsem.at[7], (peer(k + 1), dq)))
    rh_ref[me] = sh_ref[me]
    k_cols = k_ref[...].T[:, :HEADS]
    wait_for(rh_ref.at[pl.ds(0, SEQ - 1)], rsem.at[7])

    def grads_of_state(hp):
        after = get_pair(rh_ref, hp)
        db_ref[...] += dot_nt(sc_ref[hp], after)
        weighed = dot(b_in, after) * x_ref[:, cols(hp)].astype(F32)
        decayed = jnp.sum(
            after.astype(F32) * get_pair(rs_ref, hp).astype(F32), axis=0, keepdims=True)
        for j in range(2):
            head = head0 + 2 * hp + j
            sub = slice(j * N, (j + 1) * N)
            dw_ref[...] += jnp.where(
                lane == head, jnp.sum(weighed[:, sub], axis=1, keepdims=True), 0.0)
            acc_ref[9:10, :HEADS] += jnp.where(
                lane1 == head, jnp.sum(decayed[:, sub], axis=1, keepdims=True), 0.0)

    loop(PAIRS, grads_of_state)

    left = jnp.exp(cend - cum)
    d_weight = dw_ref[...] * left
    d_gap = d_weight * dt
    d_end = jnp.sum(d_gap, axis=0, keepdims=True) + jnp.exp(cend) * acc_ref[9:10, :HEADS]
    d_cum = a_ref[...] - k_cols * dt - d_gap
    tri_up = jnp.where(row_i <= col_i, 1.0, 0.0).astype(BF)
    d_log = tri_sum(tri_up, d_cum) + d_end
    d_dt = k_cols + d_weight - rate * d_log
    d_pre = d_dt / (1.0 + jnp.exp(-pre)) * SCALE
    loss = jnp.sum(jnp.sum(acc_ref[0:8], axis=0, keepdims=True), axis=1, keepdims=True)
    zero = jnp.zeros((1, HEADS), F32)
    small = jnp.concatenate([
        jnp.broadcast_to(loss * (SCALE * SCALE * 0.5), (1, HEADS)),
        jnp.sum(d_log * log_rate, axis=0, keepdims=True) * SCALE,
        jnp.sum(d_pre, axis=0, keepdims=True),
        acc_ref[8:9, :HEADS] * SCALE,
        zero, zero, zero, zero], axis=0)
    sums_ref[...] = jnp.concatenate([small, jnp.zeros_like(small)], axis=1)

    @pl.when(me != 0)
    def _():
        send(sums_ref, sroot_ref.at[me], ssem.at[14], rsem.at[14], (0, dq))

    d_bc = jnp.concatenate([db_ref[...], dc_ref[...]], axis=1) * SCALE
    dp_sum(d_bc, d_pre, p2_bc, p2_dt, r2_bc, r2_dt, f2_bc, f2_dt, 8)

    g_bc = f2_bc[...].reshape(T, 2 * N)
    g_dt = unpack_rows(f2_dt)
    none = jnp.zeros_like(g_dt)
    g_at = [
        jnp.concatenate([g_dt if i == k else none for i in range(4)], axis=1).astype(BF)
        for k in range(4)
    ]

    def weight_terms(k):
        g = lax.rem(me // 8 + k, 4)
        part = xt_ref[pl.ds(pl.multiple_of(g * 512, 512), 512), :]
        slots = pl.ds(8 * g, 8)
        ws_ref[slots, 0:PIECE, :] = dot(part, g_bc).astype(BF).reshape(8, PIECE, 2 * N)
        part = part.reshape(8, 4, 16, T)
        packed = sum(dot(part[:, i].reshape(128, T), g_at[i]) for i in range(4))
        ws_ref[slots, PIECE : PIECE + 16, :] = packed.astype(BF).reshape(8, 16, 2 * N)

        def one(i):
            o = 8 * g + lax.rem(me + i, 8)

            @pl.when(o != me)
            def _():
                send(ws_ref.at[o], rw_ref.at[me], ssem.at[12], rsem.at[12], (o, dq))

        loop(8, one)

    loop(4, weight_terms)
    rw_ref[me] = ws_ref[me]

    @pl.when(me == 0)
    def _():
        sroot_ref[0] = sums_ref[...]
        wait_for(sroot_ref.at[pl.ds(0, SEQ - 1)], rsem.at[14])
        sdp_ref[dq] = jnp.sum(sroot_ref[...], axis=0)
        for k in range(1, DP):
            send(sdp_ref.at[dq], sdp_ref.at[dq], ssem.at[15], rsem.at[15], (me, member(k)))

    wait_for(rw_ref.at[pl.ds(0, SEQ - 1)], rsem.at[12])
    total = lax.fori_loop(
        1, SEQ, lambda j, s: s + rw_ref[j].astype(F32), rw_ref[0].astype(F32))
    out_ref[me] = total.astype(BF)
    loop(SEQ - 1, lambda k: send(
        out_ref.at[me], out_ref.at[me], ssem.at[13], rsem.at[13], (peer(k + 1), dq)))

    @pl.when(me == 0)
    def _():
        wait_for(sdp_ref.at[pl.ds(0, DP - 1)], rsem.at[15])
        sfin_ref[...] = jnp.sum(sdp_ref[...], axis=0)
        loop(SEQ - 1, lambda k: send(
            sfin_ref, sfin_ref, ssem.at[16], rsem.at[16], (peer(k + 1), dq)))
        wait_for(sdp_ref.at[pl.ds(0, DP - 1)], ssem.at[15])
        wait_for(sroot_ref.at[pl.ds(0, SEQ - 1)], ssem.at[16])

    @pl.when(me != 0)
    def _():
        wait_for(sums_ref, ssem.at[14])
        wait_for(sfin_ref, rsem.at[16])

    small_ref[...] = sfin_ref[...]
    wait_for(out_ref.at[pl.ds(0, SEQ - 1)], rsem.at[13])

    for sem, ref in ((0, r_bc), (1, r_dt), (2, f_bc), (3, f_dt),
                     (8, r2_bc), (9, r2_dt), (10, f2_bc), (11, f2_dt)):
        wait_for(ref.at[pl.ds(0, DP - 1)], ssem.at[sem])
    for sem, ref in ((4, es_ref), (5, sf_ref), (6, gs_ref), (7, sh_ref), (12, ws_ref), (13, out_ref)):
        wait_for(ref.at[pl.ds(0, SEQ - 1)], ssem.at[sem])


def shards(teacher_rows, teacher_next, state_proj, step_proj, rate_log, step_bias, skip_gain):
    vmem = pl.BlockSpec(memory_space=pltpu.VMEM)
    hbm = pl.BlockSpec(memory_space=pl.ANY)

    def buf(*shape, dtype=BF):
        return pltpu.VMEM(shape, dtype)

    def f32(*shape):
        return pltpu.VMEM(shape, F32)

    dp_bufs = [
        buf(DP, 64, 2 * N), f32(DP, 32, 128), buf(DP, 64, 2 * N), f32(DP, 32, 128),
        buf(DP, 64, 2 * N), f32(DP, 32, 128),
    ]
    scratch = [
        buf(WIDTH, 2 * N), buf(WIDTH, HEADS), buf(WIDTH, T),
        *dp_bufs, *dp_bufs,
        buf(2 * T + 16, 3 * HEADS), f32(2 * HEADS, T),
        f32(PAIRS, T, 2 * N), f32(PAIRS, 8, 2 * N), buf(PAIRS, T, 2 * N), buf(PAIRS, T, 2 * N),
        buf(2 * PAIRS, T, T), f32(PAIRS, T, 2 * N), f32(PAIRS, T, 2 * N), buf(PAIRS, T, 2 * N),
        f32(T, T), f32(T, T), f32(T, N), f32(T, N), f32(2 * HEADS, T), f32(T, HEADS), f32(T, HEADS),
        f32(16, 2 * N),
        buf(SEQ, PIECE + 16, N), buf(SEQ, PIECE + 16, N),
        buf(SEQ, PIECE, N), buf(SEQ, PIECE, N), buf(SEQ, PIECE, N), buf(SEQ, PIECE, N),
        buf(SEQ, PIECE, N), buf(SEQ, PIECE, N), f32(SEQ, 8, N),
        buf(SEQ, PIECE + 16, 2 * N), buf(SEQ, PIECE + 16, 2 * N),
        f32(8, 128), f32(SEQ, 8, 128), f32(DP, 8, 128), f32(8, 128),
        pltpu.SemaphoreType.DMA((17,)), pltpu.SemaphoreType.DMA((17,)),
        pltpu.SemaphoreType.DMA((2,)),
    ]
    out, small = pl.pallas_call(
        kernel,
        out_shape=(
            jax.ShapeDtypeStruct((SEQ, PIECE + 16, 2 * N), BF),
            jax.ShapeDtypeStruct((8, 128), F32),
        ),
        in_specs=[vmem, vmem, hbm, hbm, vmem, vmem, vmem],
        out_specs=(vmem, vmem),
        scratch_shapes=scratch,
        compiler_params=pltpu.CompilerParams(
            collective_id=0, has_side_effects=True, vmem_limit_bytes=48 * 1024 * 1024),
    )(teacher_rows, teacher_next, state_proj, step_proj,
      rate_log[None], step_bias[None], skip_gain[None])
    state_grad = out[:, :PIECE].reshape(WIDTH, 2 * N).astype(F32)
    step_grad = (
        out[:, PIECE:].reshape(SEQ, 16, 4, HEADS).transpose(0, 2, 1, 3)
        .reshape(WIDTH, HEADS).astype(F32)
    )
    return (small[0, 0], state_grad, step_grad,
            small[1, :HEADS], small[2, :HEADS], small[3, :HEADS])


def solution(mesh):
    placed = (P("seq", "dp"), P("seq", "dp"), P(), P(), P(), P(), P())
    return jax.shard_map(
        shards,
        mesh=mesh,
        in_specs=placed,
        out_specs=(P(), P("dp", None), P("dp", None), P(), P(), P()),
        check_vma=False,
    )
```

time: 1170 us -> 121 us (0.10)
  waiting for transfers between devices: 732 us -> 0 us
  blocking collectives: 175 us -> 0 us
  other arithmetic: 133 us -> 1.59 us
  Pallas kernels: 0 us -> 112 us
  local copies, waits for them, and re-layouts: 74.6 us -> 6.17 us
  matrix products: 33.7 us -> 0 us
  between operations: 16.7 us -> 0.75 us
    all_gather x3 -> x0, waiting for transfers between devices: 442 us -> none  [the longest x2 394 us: entering_2(): everything = jax.tree.map(lambda part: lax.all_gather(part, axis), value)]
    psum x1 -> x0, waiting for transfers between devices: 289 us -> none  [shards(): summed = lax.psum(weight_part, 'seq')]
    select_n x64 -> x0, other arithmetic: 114 us -> none  [lap(): return jax.tree.map(lambda a, b: jnp.where(reached, a, b), new, before)]
    pallas_call x0 -> x1, Pallas kernels: none -> 112 us  [shards(): pl.pallas_call(kernel, out_shape=(jax.ShapeDtypeStruct((SEQ, PIECE + 16,...]
    all_gather x1 -> x0, blocking collectives: 95.3 us -> none  [entering_2(): everything = jax.tree.map(lambda part: lax.all_gather(part, axis), value)]
    psum x2 -> x0, blocking collectives: 79.4 us -> none  [the longest x1 65.1 us: shards(): lax.psum((partial_loss, rate_part, bias_part, skip_part), ('seq', 'dp'))]
    squeeze x64 -> x1, local copies, waits for them, and re-layouts: 44 us -> 0.52 us  [shards(): small[3, :HEADS]]
    dot_general x13 -> x0, matrix products: 33.7 us -> none  [the longest x3 9.58 us: block_output(): lax.dot_general(c_output.astype(jnp.float32), carry_state, (((1,), (1,)),...]
  transfers between devices with their start and end apart: 4 -> 0, of which waited for: 4 -> 0; matrix products, arithmetic and copies ran while one was open for 3% -> 0% of each run, Pallas kernels for 0% -> 0%
where the time goes in v1:
time: 121 us
  Pallas kernels  112 us (93%)
  local copies, waits for them, and re-layouts  6.17 us (5%)
  other arithmetic  1.59 us (1%)
    pallas_call x1, Pallas kernels, shards(): pl.pallas_call(kernel, out_shape=(jax.ShapeDtypeStruct((SEQ, PIECE + 16,...  112 us
    unnamed x12, local copies, waits for them, and re-layouts  4.47 us

profile of v1, /device:TPU:0, one launch (start us, length us, event | category | flops | bytes accessed | tf_op | source)
XLA Modules:
  0.0 120.5 jit_solution(6893494653083427893)
XLA Ops:
  0.6 0.0 copy-start.4
  0.6 0.0 copy-start.3
  0.7 0.0 copy-start.2
  0.7 0.0 copy-start
  0.7 2.1 %copy.15.st_ref = bf16[8192,64]{1,0:T(8,128)(2,1)S(1)} copy(bf16[8192,64]{0,1:T(8,128)(2,1)} %param.10) | data formatting | bytes 2097152 | tf_op args[3]
  2.8 0.0 copy-done.4
  2.8 0.0 copy-done.3
  2.8 0.0 copy-done.2
  2.8 0.0 copy-done
  2.8 0.0 copy-start.1
  2.8 1.2 %copy-done.1 = bf16[256,2048]{1,0:T(8,128)(2,1)S(1)} copy-done((bf16[256,2048]{1,0:T(8,128)(2,1)S(1)}, bf16[256,2048]{1,0:T(8,128)(2,1)}, u32[]{:S(2)}) %copy-start.1) | copy-done | bytes 1048600
  4.1 112.0 %shard_map.118 = (bf16[32,80,256]{2,1,0:T(8,128)(2,1)S(1)}, f32[8,128]{1,0:T(8,128)S(1)}) custom-call(bf16[256,2048]{1,0:T(8,128)(2,1)S(1)} %copy-done, bf16[256,2048]{1,0:T(8,128)(2,1)S(1)} %copy-done.1, bf16[8192,256]{1,0:T(8,128)(2,1)} %sp_ref.1, bf16[8192,64]{1,0:T(8,128)(2,1)S(1)} %copy.15.st_ref, f32[1,64]{1,0:T(1,128)S(1)} %bitcast.16, ...), custom_call_target="tpu_custom_call" | custom-call | tf_op jit(solution)/shard_map/pallas_call | solution.py:436
  116.1 0.5 slice.18
  116.6 0.5 slice_bitcast_fusion
  117.2 0.1 slice.19
  117.3 0.5 reshape.23
  117.8 0.1 copy.16
  117.9 1.1 copy.17
  119.0 1.5 %bitcast_convert_fusion = f32[2048,256]{1,0:T(8,128)} fusion(bf16[32,64,256]{2,1,0:T(8,128)(2,1)S(1)} %slice.19), kind=kLoop, calls=%fused_computation | loop fusion | flops 524288 | bytes 3145728 | tf_op jit(solution)/shard_map/convert_element_type | solution.py:449
  (1 shorter events, 0.0 us)
Async XLA Ops:
  0.6 2.2 %copy-start.4 = (f32[64]{0:T(128)S(1)}, f32[64]{0:T(128)}, u32[]{:S(2)}) copy-start(f32[64]{0:T(128)} %param.13) | copy-start | bytes 772
  0.6 2.2 %copy-start.3 = (f32[64]{0:T(128)S(1)}, f32[64]{0:T(128)}, u32[]{:S(2)}) copy-start(f32[64]{0:T(128)} %param.12) | copy-start | bytes 772
  0.7 2.2 %copy-start.2 = (f32[64]{0:T(128)S(1)}, f32[64]{0:T(128)}, u32[]{:S(2)}) copy-start(f32[64]{0:T(128)} %param.11) | copy-start | bytes 772
  0.7 2.2 %copy-start = (bf16[256,2048]{1,0:T(8,128)(2,1)S(1)}, bf16[256,2048]{1,0:T(8,128)(2,1)}, u32[]{:S(2)}) copy-start(bf16[256,2048]{1,0:T(8,128)(2,1)} %x_ref.1) | copy-start | bytes 3145732
  2.8 1.2 %copy-start.1 = (bf16[256,2048]{1,0:T(8,128)(2,1)S(1)}, bf16[256,2048]{1,0:T(8,128)(2,1)}, u32[]{:S(2)}) copy-start(bf16[256,2048]{1,0:T(8,128)(2,1)} %tgt_ref.1) | copy-start | bytes 3145732

commit v2 on v1

v2 whole, which is shorter than its diff:
```python
import functools

import jax
import jax.numpy as jnp
from jax import lax
from jax.experimental import pallas as pl
from jax.experimental.pallas import tpu as pltpu
from jax.sharding import PartitionSpec as P

SEQ, DP = 32, 4
T = 256
WIDTH = 2048
HEADS = 64
PAIRS = 8
N = 128
PIECE = 64
MESH = pl.DeviceIdType.MESH
BF, F32 = jnp.bfloat16, jnp.float32
SCALE = 1.0 / 8192.0


def dot(a, b):
    return jnp.dot(a, b, preferred_element_type=F32)


def dot_nt(a, b):
    return lax.dot_general(a, b, (((1,), (1,)), ((), ())), preferred_element_type=F32)


def split3(v):
    hi = v.astype(BF).astype(F32)
    rest = v - hi
    mid = rest.astype(BF).astype(F32)
    return hi, mid, rest - mid


def tri_sum(tri, v):
    return sum(dot(tri, part.astype(BF)) for part in split3(v))


def send(src, dst, send_sem, recv_sem, device):
    pltpu.make_async_remote_copy(
        src_ref=src, dst_ref=dst, send_sem=send_sem, recv_sem=recv_sem,
        device_id=device, device_id_type=MESH,
    ).start()


def wait_for(ref, sem):
    pltpu.make_async_copy(ref, ref, sem).wait()


def loop(count, body):
    lax.fori_loop(0, count, lambda k, c: (body(k), c)[1], 0)


def pack_rows(v):
    return jnp.concatenate([v[:64], v[64:]], axis=1)


def unpack_rows(ref):
    return jnp.concatenate([ref[i][:, j : j + 64] for i in range(2) for j in (0, 64)], axis=0)


def kernel(
    x_hbm, tgt_hbm, sp_ref, st_ref, rate_ref, bias_ref, skip_ref,
    wbc_ref, wdt_ref, small_ref,
    x_ref, tgt_ref, w_bc, w_dt, xt_ref,
    m1_tmp, m1_sa, m1_ra, m1_sb, m1_rb, m1_f,
    d1_tmp, d1_sa, d1_ra, d1_sb, d1_rb, d1_f,
    m2_tmp, m2_sa, m2_ra, m2_sb, m2_rb, m2_f,
    m3_tmp, m3_sa, m3_ra, m3_sb, m3_rb, m3_f,
    stack_ref, skips_ref, rows_ref, cx_ref, sk_ref, sc_ref, xdt_ref, l_ref, z_ref, err_ref, de_ref,
    sm_ref, dsc_ref, dc_ref, db_ref, k_ref, a_ref, dw_ref, acc_ref,
    ce_ref, es_ref, re_ref, sf_ref, rs_ref, gs_ref, rg_ref, sh_ref, rh_ref, dec_ref,
    wsc_ref, rwc_ref, wsb_ref, rwb_ref, sums_ref, sroot_ref, sdp_ref, sfin_ref,
    ssem, rsem, s_rsem, h_rsem, lsem, go,
):
    me, dq = lax.axis_index("seq"), lax.axis_index("dp")
    head0 = dq * (HEADS // DP)
    core = lax.rem(dq, 2)
    sibling = dq + 1 - 2 * core
    across = lax.rem(dq + 2, DP)

    def peer(k):
        return lax.rem(me + k, SEQ)

    def offset(dy, dx, dz):
        y, x, z = me // 16, lax.rem(me // 4, 4), lax.rem(me, 4)
        return lax.rem(y + dy, 2) * 16 + lax.rem(x + dx, 4) * 4 + lax.rem(z + dz, 4)

    def signal(sem, device):
        pl.semaphore_signal(sem, inc=1, device_id=device, device_id_type=MESH)

    def to_peers(start):
        def one(k):
            o = offset(1 - k // 16, lax.rem(2 + k // 4, 4), lax.rem(2 + k, 4))

            @pl.when(o != me)
            def _():
                start(o)

        loop(SEQ, one)

    own = pl.ds(pl.multiple_of(dq * WIDTH, WIDTH), WIDTH)
    load_x = pltpu.make_async_copy(x_hbm, x_ref, lsem.at[0])
    load_bc = pltpu.make_async_copy(sp_ref.at[own], w_bc, lsem.at[1])
    load_dt = pltpu.make_async_copy(st_ref.at[:, own], w_dt, lsem.at[2])
    load_tgt = pltpu.make_async_copy(tgt_hbm, tgt_ref, lsem.at[3])
    load_x.start()
    load_bc.start()
    load_dt.start()
    load_tgt.start()
    barrier = pltpu.get_barrier_semaphore()
    z_line = [(0, 0, k) for k in (1, 2, 3)]
    x_line = [(0, k, 0) for k in (1, 2, 3)]
    for k in range(1, DP):
        signal(barrier, (me, lax.rem(dq + k, DP)))
    for at in z_line + x_line + [(1, 0, 0)]:
        signal(barrier, (offset(*at), dq))
    load_x.wait()
    load_bc.wait()
    load_dt.wait()

    class DpSum:
        def __init__(self, sem, tmp, sa, ra, sb, rb, f):
            self.sem, self.tmp, self.sa, self.ra, self.sb, self.rb, self.f = sem, tmp, sa, ra, sb, rb, f

        def send(self, src, dst, step, member):
            send(src, dst, ssem.at[self.sem + step], rsem.at[self.sem + step], (me, member))

        def first(self):
            self.sa[...] = self.tmp[1 - core].astype(self.sa.dtype)
            self.send(self.sa, self.ra, 0, sibling)

        def second(self):
            wait_for(self.ra, rsem.at[self.sem])
            chip = self.tmp[core] + self.ra[...].astype(F32)
            self.tmp[core] = chip
            self.sb[...] = chip.astype(self.sb.dtype)
            self.send(self.sb, self.rb, 1, across)

        def third(self):
            wait_for(self.rb, rsem.at[self.sem + 1])
            self.f[core] = (self.tmp[core] + self.rb[...].astype(F32)).astype(self.f.dtype)
            self.send(self.f.at[core], self.f.at[core], 2, sibling)

        def last(self):
            wait_for(self.f.at[0], rsem.at[self.sem + 2])

        def sent(self):
            for step, ref in enumerate((self.sa, self.sb, self.f.at[0])):
                wait_for(ref, ssem.at[self.sem + step])

    sum_bc = DpSum(0, m1_tmp, m1_sa, m1_ra, m1_sb, m1_rb, m1_f)
    sum_dt = DpSum(3, d1_tmp, d1_sa, d1_ra, d1_sb, d1_rb, d1_f)
    sum_c = DpSum(6, m2_tmp, m2_sa, m2_ra, m2_sb, m2_rb, m2_f)
    sum_b = DpSum(9, m3_tmp, m3_sa, m3_ra, m3_sb, m3_rb, m3_f)

    x_all = x_ref[...]
    part_dt = dot_nt(x_all, w_dt[...])
    part_bc = dot(x_all, w_bc[...])
    for i in range(2):
        half = slice(128 * i, 128 * i + 128)
        d1_tmp[i] = pack_rows(part_dt[half])
        m1_tmp[i, 0:128] = part_bc[half, :N]
        m1_tmp[i, 128:256] = part_bc[half, N:]
    pl.semaphore_wait(barrier, DP - 1 + 7)
    sum_dt.first()
    sum_bc.first()
    for at in x_line:
        signal(go.at[0], (offset(*at), dq))
    sum_dt.second()
    sum_bc.second()
    pl.semaphore_wait(go.at[0], 3)
    signal(go.at[1], (offset(1, 0, 0), dq))
    sum_dt.third()
    sum_bc.third()
    sum_dt.last()
    sum_bc.last()

    b_in = m1_f[:, 0:128].reshape(T, N)
    c_out = m1_f[:, 128:256].reshape(T, N)
    pre = unpack_rows(d1_f) + bias_ref[...]
    dt = jnp.maximum(pre, 0.0) + jnp.log1p(jnp.exp(-jnp.abs(pre)))
    rate = jnp.exp(rate_ref[...])
    log_rate = -rate * dt
    row_i = lax.broadcasted_iota(jnp.int32, (T, T), 0)
    col_i = lax.broadcasted_iota(jnp.int32, (T, T), 1)
    tri = jnp.where(row_i >= col_i, 1.0, 0.0).astype(BF)
    cum = tri_sum(tri, log_rate)
    cend = cum[T - 1 : T]
    b_t = b_in.astype(F32).T.astype(BF)
    stack_ref[0:T] = jnp.concatenate(split3(cum), axis=1).astype(BF)
    stack_ref[T : 2 * T] = jnp.concatenate(split3(dt), axis=1).astype(BF)
    ce_ref[me] = jnp.concatenate([cend, cend], axis=1)
    pl.semaphore_wait(go.at[1], 1)
    loop(SEQ - 1, lambda k: send(
        ce_ref.at[me], ce_ref.at[me], ssem.at[12], rsem.at[12], (peer(k + 1), dq)))
    sel_row = lax.rem(lax.broadcasted_iota(jnp.int32, (3 * HEADS, 2 * N), 0), HEADS)
    sel_col = lax.broadcasted_iota(jnp.int32, (3 * HEADS, 2 * N), 1) // N

    def cols(hp):
        return pl.ds(pl.multiple_of(hp * 2 * N, 2 * N), 2 * N)

    def pick(hp):
        return jnp.where(sel_row == head0 + 2 * hp + sel_col, 1.0, 0.0).astype(BF)

    def send_pair(hp, src, dst, sem):
        for i in range(4):
            o = 4 * hp + i

            @pl.when(o != me)
            def _():
                send(src.at[o], dst.at[me], ssem.at[sem], rsem.at[sem], (o, dq))

    def wait_pair(hp, ref, sems):
        for i in range(4):
            o = 4 * hp + i

            @pl.when(o != me)
            def _():
                wait_for(ref.at[o], sems.at[o])

    def put_pair(ref, hp, value):
        for i in range(4):
            half, j = i % 2, i // 2
            ref[4 * hp + i] = value[
                half * PIECE : (half + 1) * PIECE, j * N : (j + 1) * N].astype(BF)

    def get_pair(ref, hp):
        v = ref[pl.ds(4 * hp, 4)]
        return jnp.concatenate([v[:2].reshape(N, N), v[2:].reshape(N, N)], axis=1)

    def increments(k):
        hp = lax.rem(me // 4 + k, PAIRS)
        wide = dot(stack_ref[...], pick(hp))
        cx, dx = wide[:T], wide[T:]
        cx_ref[hp] = cx
        xd = x_ref[:, cols(hp)].astype(F32) * dx
        xdt_ref[hp] = xd.astype(BF)
        sc = (xd * jnp.exp(cx[T - 1 : T] - cx)).astype(BF)
        sc_ref[hp] = sc
        put_pair(es_ref, hp, dot(b_t, sc))
        send_pair(hp, es_ref, re_ref, 13)

    loop(PAIRS, increments)
    re_ref[me] = es_ref[me]

    rows_ref[...] = jnp.concatenate([cum, dt], axis=1).T
    sm_ref[...] = jnp.where(row_i >= col_i, dot_nt(c_out, b_in), 0.0)
    skips_ref[...] = jnp.concatenate(
        split3(jnp.broadcast_to(skip_ref[...], (16, HEADS))), axis=1).astype(BF)

    def in_block(hp):
        sk_ref[hp] = dot(skips_ref[...], pick(hp))[:8]
        parts = []
        for j in range(2):
            cx = cx_ref[hp, :, j * N : (j + 1) * N]
            gap = jnp.concatenate([cx, cx], axis=1) - rows_ref[pl.ds(head0 + 2 * hp + j, 1), :]
            decay = jnp.exp(jnp.minimum(gap, 0.0))
            l_ref[2 * hp + j] = decay.astype(BF)
            w = (decay * sm_ref[...]).astype(BF)
            parts.append(dot(w, xdt_ref[hp, :, j * N : (j + 1) * N]))
        z_ref[hp] = jnp.concatenate(parts, axis=1)

    loop(PAIRS, in_block)
    load_tgt.wait()
    c_t = c_out.astype(F32).T.astype(BF)

    wait_for(ce_ref.at[pl.ds(0, SEQ - 1)], rsem.at[12])
    ends = jnp.concatenate(split3(ce_ref[...].reshape(SEQ, N)[:, :HEADS]), axis=1).astype(BF)
    sel_own = jnp.where(sel_row[:, :N] == head0 + me // 2, 1.0, 0.0).astype(BF)
    dec_ref[...] = jnp.exp(dot(ends, sel_own))
    wait_for(re_ref.at[pl.ds(0, SEQ - 1)], rsem.at[13])

    def forward(j, state):
        sf_ref[j] = state.astype(BF)
        return dec_ref[pl.ds(j, 1), :] * state + re_ref[j].astype(F32)

    lax.fori_loop(0, SEQ, forward, jnp.zeros((PIECE, N), F32), unroll=4)
    loop(SEQ - 1, lambda k: send(
        sf_ref.at[peer(k + 1)], rs_ref.at[me], ssem.at[14], s_rsem.at[me], (peer(k + 1), dq)))
    rs_ref[me] = sf_ref[me]

    def turn(i):
        at = pl.ds(pl.multiple_of(i * 2 * N, 2 * N), 2 * N)
        xt_ref[at, :] = x_ref[:, at].astype(F32).T.astype(BF)

    loop(PAIRS, turn)
    acc_ref[...] = jnp.zeros_like(acc_ref)

    def errors(k):
        hp = lax.rem(me // 4 + PAIRS - k, PAIRS)
        at = cols(hp)
        wait_pair(hp, rs_ref, s_rsem)
        decay = jnp.exp(cx_ref[hp])
        z = z_ref[hp] + dot(c_out, get_pair(rs_ref, hp)) * decay
        z_ref[hp] = z
        err = (z + sk_ref[hp][:1] * x_ref[:, at].astype(F32)) - tgt_ref[:, at].astype(F32)
        err_ref[hp] = err
        de = (err * decay).astype(BF)
        de_ref[hp] = de
        put_pair(gs_ref, hp, dot(c_t, de))
        send_pair(hp, gs_ref, rg_ref, 15)
        acc_ref[0:8] += jnp.sum((err * err).reshape(T // 8, 8, 2 * N), axis=0)

    loop(PAIRS, errors)
    rg_ref[me] = gs_ref[me]

    lane = lax.broadcasted_iota(jnp.int32, (T, HEADS), 1)
    lane1 = lax.broadcasted_iota(jnp.int32, (1, HEADS), 1)
    for ref in (dsc_ref, dc_ref, db_ref, k_ref, a_ref, dw_ref):
        ref[...] = jnp.zeros_like(ref)

    def grads_in_block(hp):
        at = cols(hp)
        xp = x_ref[:, at]
        err = err_ref[hp]
        errb = err.astype(BF)
        dc_ref[...] += dot_nt(de_ref[hp], get_pair(rs_ref, hp))
        rowed = err * z_ref[hp]
        skipped = jnp.sum(err * xp.astype(F32), axis=0, keepdims=True)
        for j in range(2):
            head = head0 + 2 * hp + j
            sub = slice(j * N, (j + 1) * N)
            dwd = dot_nt(errb[:, sub], xp[:, sub]) * l_ref[2 * hp + j].astype(F32)
            dsc_ref[...] += dwd * rows_ref[pl.ds(HEADS + head, 1), :]
            k_ref[pl.ds(head, 1), :] = jnp.sum(dwd * sm_ref[...], axis=0, keepdims=True)
            a_ref[...] += jnp.where(
                lane == head, jnp.sum(rowed[:, sub], axis=1, keepdims=True), 0.0)
            acc_ref[8:9, :HEADS] += jnp.where(
                lane1 == head, jnp.sum(skipped[:, sub], axis=1, keepdims=True), 0.0)

    loop(PAIRS, grads_in_block)
    dsc = jnp.where(row_i >= col_i, dsc_ref[...], 0.0)
    m2_tmp[...] = ((dc_ref[...] + dot(dsc.astype(BF), b_in)) * SCALE).reshape(2, 128, N)
    sum_c.first()
    db_ref[...] = dot(dsc.T.astype(BF), c_out)
    sum_c.second()
    k_cols = k_ref[...].T[:, :HEADS]
    sum_c.third()
    sum_c.last()

    wait_for(rg_ref.at[pl.ds(0, SEQ - 1)], rsem.at[15])

    def backward(i, state):
        j = SEQ - 1 - i
        sh_ref[j] = state.astype(BF)
        return dec_ref[pl.ds(j, 1), :] * state + rg_ref[j].astype(F32)

    lax.fori_loop(0, SEQ, backward, jnp.zeros((PIECE, N), F32), unroll=4)
    loop(SEQ - 1, lambda k: send(
        sh_ref.at[peer(k + 1)], rh_ref.at[me], ssem.at[16], h_rsem.at[me], (peer(k + 1), dq)))
    rh_ref[me] = sh_ref[me]

    g_c = m2_f[...].reshape(T, N)

    def terms_c(g):
        part = xt_ref[pl.ds(pl.multiple_of(g * 512, 512), 512), :]
        wsc_ref[pl.ds(8 * g, 8)] = dot(part, g_c).astype(BF).reshape(8, PIECE, N)

    loop(4, terms_c)
    to_peers(lambda o: send(wsc_ref.at[o], rwc_ref.at[me], ssem.at[17], rsem.at[17], (o, dq)))
    rwc_ref[me] = wsc_ref[me]

    def grads_of_state(k):
        hp = lax.rem(me // 4 + PAIRS - k, PAIRS)
        wait_pair(hp, rh_ref, h_rsem)
        after = get_pair(rh_ref, hp)
        db_ref[...] += dot_nt(sc_ref[hp], after)
        weighed = dot(b_in, after) * x_ref[:, cols(hp)].astype(F32)
        decayed = jnp.sum(
            after.astype(F32) * get_pair(rs_ref, hp).astype(F32), axis=0, keepdims=True)
        for j in range(2):
            head = head0 + 2 * hp + j
            sub = slice(j * N, (j + 1) * N)
            dw_ref[...] += jnp.where(
                lane == head, jnp.sum(weighed[:, sub], axis=1, keepdims=True), 0.0)
            acc_ref[9:10, :HEADS] += jnp.where(
                lane1 == head, jnp.sum(decayed[:, sub], axis=1, keepdims=True), 0.0)

    loop(PAIRS, grads_of_state)

    left = jnp.exp(cend - cum)
    d_weight = dw_ref[...] * left
    d_gap = d_weight * dt
    d_end = jnp.sum(d_gap, axis=0, keepdims=True) + jnp.exp(cend) * acc_ref[9:10, :HEADS]
    d_cum = a_ref[...] - k_cols * dt - d_gap
    tri_up = jnp.where(row_i <= col_i, 1.0, 0.0).astype(BF)
    d_log = tri_sum(tri_up, d_cum) + d_end
    d_dt = k_cols + d_weight - rate * d_log
    d_pre = d_dt / (1.0 + jnp.exp(-pre)) * SCALE
    for i in range(2):
        half = slice(128 * i, 128 * i + 128)
        m3_tmp[i, 0:128] = db_ref[half] * SCALE
        m3_tmp[i, 128:192] = pack_rows(d_pre[half])
    sum_b.first()
    loss = jnp.sum(jnp.sum(acc_ref[0:8], axis=0, keepdims=True), axis=1, keepdims=True)
    zero = jnp.zeros((1, HEADS), F32)
    small = jnp.concatenate([
        jnp.broadcast_to(loss * (SCALE * SCALE * 0.5), (1, HEADS)),
        jnp.sum(d_log * log_rate, axis=0, keepdims=True) * SCALE,
        jnp.sum(d_pre, axis=0, keepdims=True),
        acc_ref[8:9, :HEADS] * SCALE,
        zero, zero, zero, zero], axis=0)
    sums_ref[...] = jnp.concatenate([small, jnp.zeros_like(small)], axis=1)
    sum_b.second()

    @pl.when(me != 0)
    def _():
        send(sums_ref, sroot_ref.at[me], ssem.at[21], rsem.at[21], (0, dq))

    def total_of(ref):
        return lax.fori_loop(
            1, SEQ, lambda j, s: s + ref[j].astype(F32), ref[0].astype(F32), unroll=4).astype(BF)

    wait_for(rwc_ref.at[pl.ds(0, SEQ - 1)], rsem.at[17])
    wbc_ref[me, :, N:] = total_of(rwc_ref)
    own_c = wbc_ref.at[me, :, pl.ds(N, N)]
    to_peers(lambda o: send(own_c, own_c, ssem.at[18], rsem.at[18], (o, dq)))

    sum_b.third()
    sum_b.last()

    g_b = m3_f[:, 0:128].reshape(T, N)
    g_dt = unpack_rows(m3_f.at[:, pl.ds(128, 64)]).astype(F32).T.astype(BF)

    def terms_b(g):
        part = xt_ref[pl.ds(pl.multiple_of(g * 512, 512), 512), :]
        wsb_ref[pl.ds(8 * g, 8), 0:PIECE] = dot(part, g_b).astype(BF).reshape(8, PIECE, N)
        wide = dot(g_dt, x_ref[:, pl.ds(pl.multiple_of(g * 512, 512), 512)]).astype(BF)
        for i in range(4):
            for j in range(2):
                wsb_ref[4 * g + i + 16 * j, PIECE : PIECE + 32] = wide[
                    32 * j : 32 * j + 32, N * i : N * i + N]

    loop(4, terms_b)
    to_peers(lambda o: send(wsb_ref.at[o], rwb_ref.at[me], ssem.at[19], rsem.at[19], (o, dq)))
    rwb_ref[me] = wsb_ref[me]

    @pl.when(me == 0)
    def _():
        sroot_ref[0] = sums_ref[...]
        wait_for(sroot_ref.at[pl.ds(0, SEQ - 1)], rsem.at[21])
        sdp_ref[dq] = jnp.sum(sroot_ref[...], axis=0)
        for k in range(1, DP):
            send(sdp_ref.at[dq], sdp_ref.at[dq], ssem.at[22], rsem.at[22],
                 (me, lax.rem(dq + k, DP)))

    wait_for(rwb_ref.at[pl.ds(0, SEQ - 1)], rsem.at[19])
    total = total_of(rwb_ref)
    wbc_ref[me, :, :N] = total[:PIECE]
    own_b = wbc_ref.at[me, :, pl.ds(0, N)]
    own_dt = wdt_ref.at[pl.ds(pl.multiple_of(32 * (me // 16), 32), 32),
                        pl.ds(pl.multiple_of(N * lax.rem(me, 16), N), N)]
    own_dt[...] = total[PIECE:]

    def last_sends(o):
        send(own_b, own_b, ssem.at[20], rsem.at[20], (o, dq))
        send(own_dt, own_dt, ssem.at[24], rsem.at[24], (o, dq))

    to_peers(last_sends)

    @pl.when(me == 0)
    def _():
        wait_for(sdp_ref.at[pl.ds(0, DP - 1)], rsem.at[22])
        sfin_ref[...] = jnp.sum(sdp_ref[...], axis=0)
        loop(SEQ - 1, lambda k: send(
            sfin_ref, sfin_ref, ssem.at[23], rsem.at[23], (peer(k + 1), dq)))
        wait_for(sdp_ref.at[pl.ds(0, DP - 1)], ssem.at[22])
        wait_for(sroot_ref.at[pl.ds(0, SEQ - 1)], ssem.at[23])

    @pl.when(me != 0)
    def _():
        wait_for(sums_ref, ssem.at[21])
        wait_for(sfin_ref, rsem.at[23])

    small_ref[...] = sfin_ref[...]

    for one in (sum_bc, sum_dt, sum_c, sum_b):
        one.sent()
    pieces = pl.ds(0, SEQ - 1)
    for sem, ref in ((12, ce_ref), (13, es_ref), (14, sf_ref), (15, gs_ref), (16, sh_ref),
                     (17, wsc_ref), (18, wsc_ref), (19, wsb_ref), (20, wsc_ref)):
        wait_for(ref.at[pieces], ssem.at[sem])
    wait_for(wsb_ref.at[pieces, pl.ds(0, 32)], ssem.at[24])
    wait_for(wbc_ref.at[pieces, :, pl.ds(N, N)], rsem.at[18])
    wait_for(wbc_ref.at[pieces, :, pl.ds(0, N)], rsem.at[20])
    wait_for(rwb_ref.at[pieces, pl.ds(0, 32)], rsem.at[24])


def shards(teacher_rows, teacher_next, state_proj, step_proj, rate_log, step_bias, skip_gain):
    vmem = pl.BlockSpec(memory_space=pltpu.VMEM)
    hbm = pl.BlockSpec(memory_space=pl.ANY)

    def buf(*shape):
        return pltpu.VMEM(shape, BF)

    def f32(*shape):
        return pltpu.VMEM(shape, F32)

    def dp_bufs(rows, kind):
        return [f32(2, rows, N), *[kind(rows, N) for _ in range(4)], kind(2, rows, N)]

    scratch = [
        buf(T, WIDTH), buf(T, WIDTH), buf(WIDTH, 2 * N), buf(HEADS, WIDTH), buf(WIDTH, T),
        *dp_bufs(256, buf), *dp_bufs(64, f32), *dp_bufs(128, buf), *dp_bufs(192, buf),
        buf(2 * T, 3 * HEADS), buf(16, 3 * HEADS), f32(2 * HEADS, T),
        f32(PAIRS, T, 2 * N), f32(PAIRS, 8, 2 * N), buf(PAIRS, T, 2 * N), buf(PAIRS, T, 2 * N),
        buf(2 * PAIRS, T, T), f32(PAIRS, T, 2 * N), f32(PAIRS, T, 2 * N), buf(PAIRS, T, 2 * N),
        f32(T, T), f32(T, T), f32(T, N), f32(T, N), f32(2 * HEADS, T), f32(T, HEADS), f32(T, HEADS),
        f32(16, 2 * N),
        f32(SEQ, 1, N), *[buf(SEQ, PIECE, N) for _ in range(8)], f32(SEQ, N),
        buf(SEQ, PIECE, N), buf(SEQ, PIECE, N), buf(SEQ, PIECE + 32, N), buf(SEQ, PIECE + 32, N),
        f32(8, 128), f32(SEQ, 8, 128), f32(DP, 8, 128), f32(8, 128),
        pltpu.SemaphoreType.DMA((25,)), pltpu.SemaphoreType.DMA((25,)),
        pltpu.SemaphoreType.DMA((SEQ,)), pltpu.SemaphoreType.DMA((SEQ,)),
        pltpu.SemaphoreType.DMA((4,)), pltpu.SemaphoreType.REGULAR((2,)),
    ]
    state_grad, step_grad, small = pl.pallas_call(
        kernel,
        out_shape=(
            jax.ShapeDtypeStruct((SEQ, PIECE, 2 * N), BF),
            jax.ShapeDtypeStruct((HEADS, WIDTH), BF),
            jax.ShapeDtypeStruct((8, 128), F32),
        ),
        in_specs=[hbm, hbm, hbm, hbm, vmem, vmem, vmem],
        out_specs=(vmem, vmem, vmem),
        scratch_shapes=scratch,
        compiler_params=pltpu.CompilerParams(
            collective_id=0, has_side_effects=True, vmem_limit_bytes=52 * 1024 * 1024),
    )(teacher_rows, teacher_next, state_proj, step_proj.T,
      rate_log[None], step_bias[None], skip_gain[None])
    return (small[0, 0], state_grad.reshape(WIDTH, 2 * N).astype(F32), step_grad.astype(F32).T,
            small[1, :HEADS], small[2, :HEADS], small[3, :HEADS])


def solution(mesh):
    placed = (P("seq", "dp"), P("seq", "dp"), P(), P(), P(), P(), P())
    return jax.shard_map(
        shards,
        mesh=mesh,
        in_specs=placed,
        out_specs=(P(), P("dp", None), P("dp", None), P(), P(), P()),
        check_vma=False,
    )
```

time: 121 us -> 100 us (0.83)
  Pallas kernels: 112 us -> 93.8 us
  local copies, waits for them, and re-layouts: 6.17 us -> 2.99 us
    pallas_call x1, Pallas kernels: 112 us -> 93.8 us  [shards(): pl.pallas_call(kernel, out_shape=(jax.ShapeDtypeStruct((SEQ, PIECE, 2 * N...]
    unnamed x12 -> x6, local copies, waits for them, and re-layouts: 4.47 us -> 1.96 us
where the time goes in v2:
time: 100 us; the launch traced here: 99.8 us
  Pallas kernels  93.8 us (94%)
  local copies, waits for them, and re-layouts  2.99 us (3%)
  other arithmetic  2.37 us (2%)
    pallas_call x1, Pallas kernels, shards(): pl.pallas_call(kernel, out_shape=(jax.ShapeDtypeStruct((SEQ, PIECE, 2 * N...  93.8 us

profile of v2, /device:TPU:0, one launch (start us, length us, event | category | flops | bytes accessed | tf_op | source)
XLA Modules:
  0.0 99.8 jit_solution(7565838963319701909)
XLA Ops:
  0.6 0.0 copy-start
  0.6 0.6 copy-done
  1.3 0.0 copy-start.1
  1.3 0.7 copy-done.1
  1.9 0.0 copy-start.2
  1.9 0.7 copy-done.2
  2.6 93.8 %shard_map.118 = (bf16[32,64,256]{2,1,0:T(8,128)(2,1)S(1)}, bf16[64,2048]{1,0:T(8,128)(2,1)S(1)}, f32[8,128]{1,0:T(8,128)S(1)}) custom-call(bf16[256,2048]{1,0:T(8,128)(2,1)} %x_hbm.1, bf16[256,2048]{1,0:T(8,128)(2,1)} %tgt_hbm.1, bf16[8192,256]{1,0:T(8,128)(2,1)} %sp_ref.1, bf16[64,8192]{1,0:T(8,128)(2,1)} %bitcast.19, f32[1,64]{1,0:T(1,128)S(1)} %bitcast.16, ...), custom_call_target="tpu_custom_call" | custom-call | tf_op jit(solution)/shard_map/pallas_call | solution.py:520
  96.4 0.5 slice_bitcast_fusion
  96.9 0.5 slice.12
  97.5 1.5 %bitcast_convert_fusion = f32[2048,256]{1,0:T(8,128)} fusion(bf16[32,64,256]{2,1,0:T(8,128)(2,1)S(1)} %get-tuple-element.10), kind=kLoop, calls=%fused_computation | loop fusion | flops 524288 | bytes 3145728 | tf_op jit(solution)/shard_map/convert_element_type | solution.py:534
  99.0 0.8 convert_bitcast_fusion
Async XLA Ops:
  0.6 0.7 copy-start
  1.3 0.7 copy-start.1
  1.9 0.7 copy-start.2

commit v3 on v2

--- a/solution.py
+++ b/solution.py
@@ -62,18 +62,19 @@
 
 
 def kernel(
-    x_hbm, tgt_hbm, sp_ref, st_ref, rate_ref, bias_ref, skip_ref,
+    x_hbm, tgt_hbm, sp_ref, st_ref, heads_ref,
     wbc_ref, wdt_ref, small_ref,
     x_ref, tgt_ref, w_bc, w_dt, xt_ref,
+    m0_tmp, m0_sa, m0_ra, m0_sb, m0_rb, m0_f,
     m1_tmp, m1_sa, m1_ra, m1_sb, m1_rb, m1_f,
     d1_tmp, d1_sa, d1_ra, d1_sb, d1_rb, d1_f,
     m2_tmp, m2_sa, m2_ra, m2_sb, m2_rb, m2_f,
     m3_tmp, m3_sa, m3_ra, m3_sb, m3_rb, m3_f,
-    stack_ref, skips_ref, rows_ref, cx_ref, sk_ref, sc_ref, xdt_ref, l_ref, z_ref, err_ref, de_ref,
+    weight_ref, stack_ref, skips_ref, rows_ref, cx_ref, sk_ref, sc_ref, l_ref, z_ref, err_ref, de_ref,
     sm_ref, dsc_ref, dc_ref, db_ref, k_ref, a_ref, dw_ref, acc_ref,
     ce_ref, es_ref, re_ref, sf_ref, rs_ref, gs_ref, rg_ref, sh_ref, rh_ref, dec_ref,
-    wsc_ref, rwc_ref, wsb_ref, rwb_ref, sums_ref, sroot_ref, sdp_ref, sfin_ref,
-    ssem, rsem, s_rsem, h_rsem, lsem, go,
+    z1_s, z1_r, x1_s, x1_r, z2_s, z2_r, x2_s, x2_r, wsb_ref, rwb_ref, sums_ref, sroot_ref, sdp_ref, sfin_ref,
+    ssem, rsem, s_rsem, h_rsem, w_rsem, lsem, go,
 ):
     me, dq = lax.axis_index("seq"), lax.axis_index("dp")
     head0 = dq * (HEADS // DP)
@@ -101,6 +102,13 @@
 
         loop(SEQ, one)
 
+    barrier = pltpu.get_barrier_semaphore()
+    z_line = [(0, 0, k) for k in (1, 2, 3)]
+    x_line = [(0, k, 0) for k in (1, 2, 3)]
+    for k in range(1, DP):
+        signal(barrier, (me, lax.rem(dq + k, DP)))
+    for at in z_line + x_line + [(1, 0, 0)]:
+        signal(barrier, (offset(*at), dq))
     own = pl.ds(pl.multiple_of(dq * WIDTH, WIDTH), WIDTH)
     load_x = pltpu.make_async_copy(x_hbm, x_ref, lsem.at[0])
     load_bc = pltpu.make_async_copy(sp_ref.at[own], w_bc, lsem.at[1])
@@ -110,13 +118,6 @@
     load_bc.start()
     load_dt.start()
     load_tgt.start()
-    barrier = pltpu.get_barrier_semaphore()
-    z_line = [(0, 0, k) for k in (1, 2, 3)]
-    x_line = [(0, k, 0) for k in (1, 2, 3)]
-    for k in range(1, DP):
-        signal(barrier, (me, lax.rem(dq + k, DP)))
-    for at in z_line + x_line + [(1, 0, 0)]:
-        signal(barrier, (offset(*at), dq))
     load_x.wait()
     load_bc.wait()
     load_dt.wait()
@@ -151,7 +152,8 @@
             for step, ref in enumerate((self.sa, self.sb, self.f.at[0])):
                 wait_for(ref, ssem.at[self.sem + step])
 
-    sum_bc = DpSum(0, m1_tmp, m1_sa, m1_ra, m1_sb, m1_rb, m1_f)
+    sum_b1 = DpSum(0, m0_tmp, m0_sa, m0_ra, m0_sb, m0_rb, m0_f)
+    sum_c1 = DpSum(25, m1_tmp, m1_sa, m1_ra, m1_sb, m1_rb, m1_f)
     sum_dt = DpSum(3, d1_tmp, d1_sa, d1_ra, d1_sb, d1_rb, d1_f)
     sum_c = DpSum(6, m2_tmp, m2_sa, m2_ra, m2_sb, m2_rb, m2_f)
     sum_b = DpSum(9, m3_tmp, m3_sa, m3_ra, m3_sb, m3_rb, m3_f)
@@ -162,27 +164,28 @@
     for i in range(2):
         half = slice(128 * i, 128 * i + 128)
         d1_tmp[i] = pack_rows(part_dt[half])
-        m1_tmp[i, 0:128] = part_bc[half, :N]
-        m1_tmp[i, 128:256] = part_bc[half, N:]
+        m0_tmp[i] = part_bc[half, :N]
+        m1_tmp[i] = part_bc[half, N:]
     pl.semaphore_wait(barrier, DP - 1 + 7)
     sum_dt.first()
-    sum_bc.first()
+    sum_b1.first()
+    sum_c1.first()
     for at in x_line:
         signal(go.at[0], (offset(*at), dq))
     sum_dt.second()
-    sum_bc.second()
+    sum_b1.second()
+    sum_c1.second()
     pl.semaphore_wait(go.at[0], 3)
     signal(go.at[1], (offset(1, 0, 0), dq))
     sum_dt.third()
-    sum_bc.third()
+    sum_b1.third()
     sum_dt.last()
-    sum_bc.last()
-
-    b_in = m1_f[:, 0:128].reshape(T, N)
-    c_out = m1_f[:, 128:256].reshape(T, N)
-    pre = unpack_rows(d1_f) + bias_ref[...]
+    sum_b1.last()
+
+    b_in = m0_f[...].reshape(T, N)
+    pre = unpack_rows(d1_f) + heads_ref[1:2]
     dt = jnp.maximum(pre, 0.0) + jnp.log1p(jnp.exp(-jnp.abs(pre)))
-    rate = jnp.exp(rate_ref[...])
+    rate = jnp.exp(heads_ref[0:1])
     log_rate = -rate * dt
     row_i = lax.broadcasted_iota(jnp.int32, (T, T), 0)
     col_i = lax.broadcasted_iota(jnp.int32, (T, T), 1)
@@ -190,8 +193,9 @@
     cum = tri_sum(tri, log_rate)
     cend = cum[T - 1 : T]
     b_t = b_in.astype(F32).T.astype(BF)
-    stack_ref[0:T] = jnp.concatenate(split3(cum), axis=1).astype(BF)
-    stack_ref[T : 2 * T] = jnp.concatenate(split3(dt), axis=1).astype(BF)
+    weight = dt * jnp.exp(cend - cum)
+    high = weight.astype(BF).astype(F32)
+    weight_ref[...] = jnp.concatenate([high, weight - high], axis=1).astype(BF)
     ce_ref[me] = jnp.concatenate([cend, cend], axis=1)
     pl.semaphore_wait(go.at[1], 1)
     loop(SEQ - 1, lambda k: send(
@@ -233,12 +237,8 @@
 
     def increments(k):
         hp = lax.rem(me // 4 + k, PAIRS)
-        wide = dot(stack_ref[...], pick(hp))
-        cx, dx = wide[:T], wide[T:]
-        cx_ref[hp] = cx
-        xd = x_ref[:, cols(hp)].astype(F32) * dx
-        xdt_ref[hp] = xd.astype(BF)
-        sc = (xd * jnp.exp(cx[T - 1 : T] - cx)).astype(BF)
+        wide = dot(weight_ref[...], pick(hp)[: 2 * HEADS])
+        sc = (x_ref[:, cols(hp)].astype(F32) * wide).astype(BF)
         sc_ref[hp] = sc
         put_pair(es_ref, hp, dot(b_t, sc))
         send_pair(hp, es_ref, re_ref, 13)
@@ -246,21 +246,29 @@
     loop(PAIRS, increments)
     re_ref[me] = es_ref[me]
 
+    sum_c1.third()
+    stack_ref[0:T] = jnp.concatenate(split3(cum), axis=1).astype(BF)
+    stack_ref[T : 2 * T] = jnp.concatenate(split3(dt), axis=1).astype(BF)
     rows_ref[...] = jnp.concatenate([cum, dt], axis=1).T
+    sum_c1.last()
+    c_out = m1_f[...].reshape(T, N)
     sm_ref[...] = jnp.where(row_i >= col_i, dot_nt(c_out, b_in), 0.0)
     skips_ref[...] = jnp.concatenate(
-        split3(jnp.broadcast_to(skip_ref[...], (16, HEADS))), axis=1).astype(BF)
+        split3(jnp.broadcast_to(heads_ref[2:3], (16, HEADS))), axis=1).astype(BF)
 
     def in_block(hp):
         sk_ref[hp] = dot(skips_ref[...], pick(hp))[:8]
+        wide = dot(stack_ref[...], pick(hp))
+        cx_ref[hp] = wide[:T]
+        xd = (x_ref[:, cols(hp)].astype(F32) * wide[T:]).astype(BF)
         parts = []
         for j in range(2):
-            cx = cx_ref[hp, :, j * N : (j + 1) * N]
+            cx = wide[:T, j * N : (j + 1) * N]
             gap = jnp.concatenate([cx, cx], axis=1) - rows_ref[pl.ds(head0 + 2 * hp + j, 1), :]
             decay = jnp.exp(jnp.minimum(gap, 0.0))
             l_ref[2 * hp + j] = decay.astype(BF)
             w = (decay * sm_ref[...]).astype(BF)
-            parts.append(dot(w, xdt_ref[hp, :, j * N : (j + 1) * N]))
+            parts.append(dot(w, xd[:, j * N : (j + 1) * N]))
         z_ref[hp] = jnp.concatenate(parts, axis=1)
 
     loop(PAIRS, in_block)
@@ -338,9 +346,6 @@
     db_ref[...] = dot(dsc.T.astype(BF), c_out)
     sum_c.second()
     k_cols = k_ref[...].T[:, :HEADS]
-    sum_c.third()
-    sum_c.last()
-
     wait_for(rg_ref.at[pl.ds(0, SEQ - 1)], rsem.at[15])
 
     def backward(i, state):
@@ -353,15 +358,68 @@
         sh_ref.at[peer(k + 1)], rh_ref.at[me], ssem.at[16], h_rsem.at[me], (peer(k + 1), dq)))
     rh_ref[me] = sh_ref[me]
 
+    sum_c.third()
+    sum_c.last()
+
+    my_y, my_x, my_z = me // 16, lax.rem(me // 4, 4), lax.rem(me, 4)
     g_c = m2_f[...].reshape(T, N)
-
-    def terms_c(g):
-        part = xt_ref[pl.ds(pl.multiple_of(g * 512, 512), 512), :]
-        wsc_ref[pl.ds(8 * g, 8)] = dot(part, g_c).astype(BF).reshape(8, PIECE, N)
-
-    loop(4, terms_c)
-    to_peers(lambda o: send(wsc_ref.at[o], rwc_ref.at[me], ssem.at[17], rsem.at[17], (o, dq)))
-    rwc_ref[me] = wsc_ref[me]
+    for g in range(4):
+        term = dot(xt_ref[512 * g : 512 * g + 512, :], g_c).astype(BF).reshape(8, PIECE, N)
+        for i in range(8):
+            y, x, z = g // 2, 2 * (g % 2) + i // 4, i % 4
+            z1_s[z, 4 * y + x] = term[i, :32]
+            x1_s[x, 4 * y + z] = term[i, 32:]
+    for k in range(1, 4):
+        to = lax.rem(my_z + k, 4)
+        send(z1_s.at[to], z1_r.at[my_z], ssem.at[17], rsem.at[17], (offset(0, 0, k), dq))
+        to = lax.rem(my_x + k, 4)
+        send(x1_s.at[to], x1_r.at[my_x], ssem.at[18], rsem.at[18], (offset(0, k, 0), dq))
+    z1_r[my_z] = z1_s[my_z]
+    x1_r[my_x] = x1_s[my_x]
+    planes = [(dy, d) for dy in (1, 0) for d in (2, 1, 3, 0)][:7]
+
+    def on_plane(dy, mine, d):
+        return 4 * lax.rem(my_y + dy, 2) + lax.rem(mine + d, 4)
+
+    def lines_to_planes():
+        wait_for(z1_r.at[pl.ds(0, 3)], rsem.at[17])
+        z2_s[...] = sum(z1_r[i].astype(F32) for i in range(4)).astype(BF)
+        wait_for(x1_r.at[pl.ds(0, 3)], rsem.at[18])
+        x2_s[...] = sum(x1_r[i].astype(F32) for i in range(4)).astype(BF)
+        at_z, at_x = on_plane(0, my_x, 0), on_plane(0, my_z, 0)
+        for dy, d in planes:
+            send(z2_s.at[on_plane(dy, my_x, d)], z2_r.at[at_z],
+                 ssem.at[28], rsem.at[28], (offset(dy, d, 0), dq))
+            send(x2_s.at[on_plane(dy, my_z, d)], x2_r.at[at_x],
+                 ssem.at[29], rsem.at[29], (offset(dy, 0, d), dq))
+        z2_r[at_z] = z2_s[at_z]
+        x2_r[at_x] = x2_s[at_x]
+
+    def half_of(piece, i):
+        return wbc_ref.at[piece, pl.ds(32 * i, 32), pl.ds(N, N)]
+
+    def planes_back():
+        wait_for(z2_r.at[pl.ds(0, 7)], rsem.at[28])
+        wait_for(x2_r.at[pl.ds(0, 7)], rsem.at[29])
+        wbc_ref[me, 0:32, N:] = sum(z2_r[i].astype(F32) for i in range(8)).astype(BF)
+        wbc_ref[me, 32:64, N:] = sum(x2_r[i].astype(F32) for i in range(8)).astype(BF)
+        for dy, d in planes:
+            send(half_of(me, 0), half_of(me, 0), ssem.at[30], rsem.at[30], (offset(dy, d, 0), dq))
+            send(half_of(me, 1), half_of(me, 1), ssem.at[31], rsem.at[31], (offset(dy, 0, d), dq))
+
+    def lines_back():
+        wait_for(wbc_ref.at[pl.ds(0, 7), pl.ds(0, 32), pl.ds(N, N)], rsem.at[30])
+        wait_for(wbc_ref.at[pl.ds(0, 7), pl.ds(0, 32), pl.ds(N, N)], rsem.at[31])
+
+        def one(i):
+            y, other = i // 4, lax.rem(i, 4)
+            for k in range(1, 4):
+                piece = half_of(16 * y + 4 * other + my_z, 0)
+                send(piece, piece, ssem.at[32], rsem.at[32], (offset(0, 0, k), dq))
+                piece = half_of(16 * y + 4 * my_x + other, 1)
+                send(piece, piece, ssem.at[33], rsem.at[33], (offset(0, k, 0), dq))
+
+        loop(8, one)
 
     def grads_of_state(k):
         hp = lax.rem(me // 4 + PAIRS - k, PAIRS)
@@ -410,15 +468,7 @@
     def _():
         send(sums_ref, sroot_ref.at[me], ssem.at[21], rsem.at[21], (0, dq))
 
-    def total_of(ref):
-        return lax.fori_loop(
-            1, SEQ, lambda j, s: s + ref[j].astype(F32), ref[0].astype(F32), unroll=4).astype(BF)
-
-    wait_for(rwc_ref.at[pl.ds(0, SEQ - 1)], rsem.at[17])
-    wbc_ref[me, :, N:] = total_of(rwc_ref)
-    own_c = wbc_ref.at[me, :, pl.ds(N, N)]
-    to_peers(lambda o: send(own_c, own_c, ssem.at[18], rsem.at[18], (o, dq)))
-
+    lines_to_planes()
     sum_b.third()
     sum_b.last()
 
@@ -435,8 +485,9 @@
                     32 * j : 32 * j + 32, N * i : N * i + N]
 
     loop(4, terms_b)
-    to_peers(lambda o: send(wsb_ref.at[o], rwb_ref.at[me], ssem.at[19], rsem.at[19], (o, dq)))
+    to_peers(lambda o: send(wsb_ref.at[o], rwb_ref.at[me], ssem.at[19], w_rsem.at[me], (o, dq)))
     rwb_ref[me] = wsb_ref[me]
+    planes_back()
 
     @pl.when(me == 0)
     def _():
@@ -447,8 +498,18 @@
             send(sdp_ref.at[dq], sdp_ref.at[dq], ssem.at[22], rsem.at[22],
                  (me, lax.rem(dq + k, DP)))
 
-    wait_for(rwb_ref.at[pl.ds(0, SEQ - 1)], rsem.at[19])
-    total = total_of(rwb_ref)
+    lines_back()
+
+    def add(k, so_far):
+        o = offset(1 + k // 16, lax.rem(2 + 3 * (k // 4), 4), lax.rem(2 + 3 * k, 4))
+
+        @pl.when(o != me)
+        def _():
+            wait_for(rwb_ref.at[o], w_rsem.at[o])
+
+        return so_far + rwb_ref[o].astype(F32)
+
+    total = lax.fori_loop(0, SEQ, add, jnp.zeros((PIECE + 32, N), F32)).astype(BF)
     wbc_ref[me, :, :N] = total[:PIECE]
     own_b = wbc_ref.at[me, :, pl.ds(0, N)]
     own_dt = wdt_ref.at[pl.ds(pl.multiple_of(32 * (me // 16), 32), 32),
@@ -477,16 +538,39 @@
 
     small_ref[...] = sfin_ref[...]
 
-    for one in (sum_bc, sum_dt, sum_c, sum_b):
+    for one in (sum_b1, sum_c1, sum_dt, sum_c, sum_b):
         one.sent()
     pieces = pl.ds(0, SEQ - 1)
     for sem, ref in ((12, ce_ref), (13, es_ref), (14, sf_ref), (15, gs_ref), (16, sh_ref),
-                     (17, wsc_ref), (18, wsc_ref), (19, wsb_ref), (20, wsc_ref)):
+                     (19, wsb_ref), (20, sf_ref)):
         wait_for(ref.at[pieces], ssem.at[sem])
     wait_for(wsb_ref.at[pieces, pl.ds(0, 32)], ssem.at[24])
-    wait_for(wbc_ref.at[pieces, :, pl.ds(N, N)], rsem.at[18])
+    for i in range(2):
+        wait_for(z1_s.at[pl.ds(0, 3)], ssem.at[17 + i])
+        wait_for(z2_s.at[pl.ds(0, 7)], ssem.at[28 + i])
+        wait_for(z2_s.at[pl.ds(0, 7)], ssem.at[30 + i])
+        wait_for(z1_s.at[pl.ds(0, 3)], ssem.at[32 + i])
+        wait_for(z1_s.at[pl.ds(0, 3)], rsem.at[32 + i])
     wait_for(wbc_ref.at[pieces, :, pl.ds(0, N)], rsem.at[20])
     wait_for(rwb_ref.at[pieces, pl.ds(0, 32)], rsem.at[24])
+
+
+def widen(wbc_ref, wdt_ref, small_ref, bc_hbm, dt_hbm, loss_ref, *rest):
+    sums, (bc_ref, dt_ref, sem) = rest[:3], rest[3:]
+    copies = []
+    for i in range(4):
+        bc_ref[i] = wbc_ref[8 * i : 8 * i + 8].astype(F32).reshape(512, 2 * N)
+        copies.append(pltpu.make_async_copy(
+            bc_ref.at[i], bc_hbm.at[pl.ds(512 * i, 512)], sem.at[i]))
+        copies[-1].start()
+    dt_ref[...] = wdt_ref[...].astype(F32)
+    copies.append(pltpu.make_async_copy(dt_ref, dt_hbm, sem.at[4]))
+    copies[-1].start()
+    loss_ref[...] = small_ref[0:1, 0:1]
+    for i, ref in enumerate(sums):
+        ref[...] = small_ref[i + 1 : i + 2, :HEADS]
+    for one in copies:
+        one.wait()
 
 
 def shards(teacher_rows, teacher_next, state_proj, step_proj, rate_log, step_bias, skip_gain):
@@ -500,21 +584,23 @@
         return pltpu.VMEM(shape, F32)
 
     def dp_bufs(rows, kind):
-        return [f32(2, rows, N), *[kind(rows, N) for _ in range(4)], kind(2, rows, N)]
+        return [f32(2, rows, N), kind(rows, N), kind(rows, N), buf(rows, N), buf(rows, N),
+                kind(2, rows, N)]
 
     scratch = [
         buf(T, WIDTH), buf(T, WIDTH), buf(WIDTH, 2 * N), buf(HEADS, WIDTH), buf(WIDTH, T),
-        *dp_bufs(256, buf), *dp_bufs(64, f32), *dp_bufs(128, buf), *dp_bufs(192, buf),
-        buf(2 * T, 3 * HEADS), buf(16, 3 * HEADS), f32(2 * HEADS, T),
-        f32(PAIRS, T, 2 * N), f32(PAIRS, 8, 2 * N), buf(PAIRS, T, 2 * N), buf(PAIRS, T, 2 * N),
+        *dp_bufs(128, buf), *dp_bufs(128, buf), *dp_bufs(64, f32), *dp_bufs(128, buf), *dp_bufs(192, buf),
+        buf(T, 2 * HEADS), buf(2 * T, 3 * HEADS), buf(16, 3 * HEADS), f32(2 * HEADS, T),
+        f32(PAIRS, T, 2 * N), f32(PAIRS, 8, 2 * N), buf(PAIRS, T, 2 * N),
         buf(2 * PAIRS, T, T), f32(PAIRS, T, 2 * N), f32(PAIRS, T, 2 * N), buf(PAIRS, T, 2 * N),
         f32(T, T), f32(T, T), f32(T, N), f32(T, N), f32(2 * HEADS, T), f32(T, HEADS), f32(T, HEADS),
         f32(16, 2 * N),
         f32(SEQ, 1, N), *[buf(SEQ, PIECE, N) for _ in range(8)], f32(SEQ, N),
-        buf(SEQ, PIECE, N), buf(SEQ, PIECE, N), buf(SEQ, PIECE + 32, N), buf(SEQ, PIECE + 32, N),
+        *[buf(4, 8, 32, N) for _ in range(4)], *[buf(8, 32, N) for _ in range(4)],
+        buf(SEQ, PIECE + 32, N), buf(SEQ, PIECE + 32, N),
         f32(8, 128), f32(SEQ, 8, 128), f32(DP, 8, 128), f32(8, 128),
-        pltpu.SemaphoreType.DMA((25,)), pltpu.SemaphoreType.DMA((25,)),
-        pltpu.SemaphoreType.DMA((SEQ,)), pltpu.SemaphoreType.DMA((SEQ,)),
+        pltpu.SemaphoreType.DMA((34,)), pltpu.SemaphoreType.DMA((34,)),
+        *[pltpu.SemaphoreType.DMA((SEQ,)) for _ in range(3)],
         pltpu.SemaphoreType.DMA((4,)), pltpu.SemaphoreType.REGULAR((2,)),
     ]
     state_grad, step_grad, small = pl.pallas_call(
@@ -524,15 +610,27 @@
             jax.ShapeDtypeStruct((HEADS, WIDTH), BF),
             jax.ShapeDtypeStruct((8, 128), F32),
         ),
-        in_specs=[hbm, hbm, hbm, hbm, vmem, vmem, vmem],
+        in_specs=[hbm, hbm, hbm, hbm, vmem],
         out_specs=(vmem, vmem, vmem),
         scratch_shapes=scratch,
         compiler_params=pltpu.CompilerParams(
             collective_id=0, has_side_effects=True, vmem_limit_bytes=52 * 1024 * 1024),
     )(teacher_rows, teacher_next, state_proj, step_proj.T,
-      rate_log[None], step_bias[None], skip_gain[None])
-    return (small[0, 0], state_grad.reshape(WIDTH, 2 * N).astype(F32), step_grad.astype(F32).T,
-            small[1, :HEADS], small[2, :HEADS], small[3, :HEADS])
+      jnp.stack([rate_log, step_bias, skip_gain]))
+    heads = jax.ShapeDtypeStruct((1, HEADS), F32)
+    state_grad, step_grad, loss, *sums = pl.pallas_call(
+        widen,
+        out_shape=(
+            jax.ShapeDtypeStruct((WIDTH, 2 * N), F32),
+            jax.ShapeDtypeStruct((HEADS, WIDTH), F32),
+            jax.ShapeDtypeStruct((1, 1), F32), heads, heads, heads,
+        ),
+        in_specs=[vmem] * 3,
+        out_specs=(hbm, hbm, vmem, vmem, vmem, vmem),
+        scratch_shapes=[f32(4, 512, 2 * N), f32(HEADS, WIDTH), pltpu.SemaphoreType.DMA((5,))],
+        compiler_params=pltpu.CompilerParams(vmem_limit_bytes=16 * 1024 * 1024),
+    )(state_grad, step_grad, small)
+    return (loss[0, 0], state_grad, step_grad.T, *(v[0] for v in sums))
 
 
 def solution(mesh):

time: 100 us -> 92.4 us (0.924)
  Pallas kernels: 93.8 us -> 90.5 us
  local copies, waits for them, and re-layouts: 2.99 us -> 0 us
  other arithmetic: 2.37 us -> 0.7 us
    pallas_call x1, Pallas kernels: 93.8 us -> 88.4 us  [shards(): pl.pallas_call(kernel, out_shape=(jax.ShapeDtypeStruct((SEQ, PIECE, 2 * N...]
    pallas_call x0 -> x1, Pallas kernels: none -> 2.09 us  [shards(): pl.pallas_call(widen, out_shape=(jax.ShapeDtypeStruct((WIDTH, 2 * N), F32...]
    unnamed x6 -> x0, local copies, waits for them, and re-layouts: 1.96 us -> none
    convert_element_type x1 -> x0, other arithmetic: 1.54 us -> none  [shards(): state_grad.reshape(WIDTH, 2 * N).astype(F32)]
where the time goes in v3:
time: 92.4 us; the launch traced here: 91.8 us
  Pallas kernels  90.5 us (98%)
    pallas_call x1, Pallas kernels, shards(): pl.pallas_call(kernel, out_shape=(jax.ShapeDtypeStruct((SEQ, PIECE, 2 * N...  88.4 us
    pallas_call x1, Pallas kernels, shards(): pl.pallas_call(widen, out_shape=(jax.ShapeDtypeStruct((WIDTH, 2 * N), F32...  2.09 us

profile of v3, /device:TPU:0, one launch (start us, length us, event | category | flops | bytes accessed | tf_op | source)
XLA Modules:
  0.0 91.8 jit_solution(9065626507637183072)
XLA Ops:
  0.6 0.7 pad_maximum_fusion.heads_ref
  1.3 88.4 %shard_map.118 = (bf16[32,64,256]{2,1,0:T(8,128)(2,1)S(1)}, bf16[64,2048]{1,0:T(8,128)(2,1)S(1)}, f32[8,128]{1,0:T(8,128)S(1)}) custom-call(bf16[256,2048]{1,0:T(8,128)(2,1)} %x_hbm.1, bf16[256,2048]{1,0:T(8,128)(2,1)} %tgt_hbm.1, bf16[8192,256]{1,0:T(8,128)(2,1)} %sp_ref.1, bf16[64,8192]{1,0:T(8,128)(2,1)} %bitcast.9, f32[3,64]{1,0:T(4,128)S(1)} %pad_maximum_fusion.heads_ref), custom_call_target="tpu_custom_call" | custom-call | tf_op jit(solution)/shard_map/pallas_call | solution.py:606
  89.7 2.1 %shard_map.119 = (f32[2048,256]{1,0:T(8,128)}, f32[64,2048]{1,0:T(8,128)}, f32[1,1]{1,0:T(1,128)}, f32[1,64]{1,0:T(1,128)}, f32[1,64]{1,0:T(1,128)}, /*index=5*/f32[1,64]{1,0:T(1,128)}) custom-call(bf16[32,64,256]{2,1,0:T(8,128)(2,1)S(1)} %get-tuple-element.15.wbc_ref, bf16[64,2048]{1,0:T(8,128)(2,1)S(1)} %get-tuple-element.16.wdt_ref, ...), custom_call_target="tpu_custom_call" | custom-call | tf_op jit(solution)/shard_map/pallas_call | solution.py:621

commit v4 on v3

--- a/solution.py
+++ b/solution.py
@@ -14,6 +14,7 @@
 PAIRS = 8
 N = 128
 PIECE = 64
+PART = 32
 MESH = pl.DeviceIdType.MESH
 BF, F32 = jnp.bfloat16, jnp.float32
 SCALE = 1.0 / 8192.0
@@ -74,7 +75,7 @@
     sm_ref, dsc_ref, dc_ref, db_ref, k_ref, a_ref, dw_ref, acc_ref,
     ce_ref, es_ref, re_ref, sf_ref, rs_ref, gs_ref, rg_ref, sh_ref, rh_ref, dec_ref,
     z1_s, z1_r, x1_s, x1_r, z2_s, z2_r, x2_s, x2_r, wsb_ref, rwb_ref, sums_ref, sroot_ref, sdp_ref, sfin_ref,
-    ssem, rsem, s_rsem, h_rsem, w_rsem, lsem, go,
+    ssem, rsem, g_rsem, s_rsem, h_rsem, w_rsem, lsem, go,
 ):
     me, dq = lax.axis_index("seq"), lax.axis_index("dp")
     head0 = dq * (HEADS // DP)
@@ -94,13 +95,10 @@
 
     def to_peers(start):
         def one(k):
-            o = offset(1 - k // 16, lax.rem(2 + k // 4, 4), lax.rem(2 + k, 4))
-
-            @pl.when(o != me)
-            def _():
-                start(o)
-
-        loop(SEQ, one)
+            k = k + 1
+            start(peer(k))
+
+        loop(SEQ - 1, one)
 
     barrier = pltpu.get_barrier_semaphore()
     z_line = [(0, 0, k) for k in (1, 2, 3)]
@@ -209,42 +207,67 @@
     def pick(hp):
         return jnp.where(sel_row == head0 + 2 * hp + sel_col, 1.0, 0.0).astype(BF)
 
-    def send_pair(hp, src, dst, sem):
-        for i in range(4):
-            o = 4 * hp + i
+    def pair_of(group, k):
+        return 4 * group + lax.rem(me // 8 + k, 4)
+
+    def each_of(hp, body):
+        def one(i):
+            at = 8 * hp + lax.rem(me + i, 8)
+            o = lax.rem(at, SEQ)
 
             @pl.when(o != me)
             def _():
-                send(src.at[o], dst.at[me], ssem.at[sem], rsem.at[sem], (o, dq))
+                body(at, o)
+
+        loop(8, one)
+
+    def send_pair(hp, src, dst, sem):
+        each_of(hp, lambda at, o: send(
+            src.at[at], dst.at[SEQ * (hp // 4) + me],
+            ssem.at[sem], g_rsem.at[2 * (sem - 13) + hp // 4], (o, dq)))
 
     def wait_pair(hp, ref, sems):
-        for i in range(4):
-            o = 4 * hp + i
-
-            @pl.when(o != me)
-            def _():
-                wait_for(ref.at[o], sems.at[o])
+        mine = (SEQ * (hp // 4) + me) // 8 == hp
+
+        @pl.when(mine)
+        def _():
+            wait_for(ref.at[pl.ds(8 * hp, 7)], sems.at[hp])
+
+        @pl.when(jnp.logical_not(mine))
+        def _():
+            wait_for(ref.at[pl.ds(8 * hp, 8)], sems.at[hp])
+
+    def send_all(group, src, dst, sem, sems):
+        def one(k):
+            o = peer(k + 1)
+            send(src.at[SEQ * group + o], dst.at[SEQ * group + me],
+                 ssem.at[sem], sems.at[(SEQ * group + me) // 8], (o, dq))
+
+        loop(SEQ - 1, one)
+        dst[SEQ * group + me] = src[SEQ * group + me]
 
     def put_pair(ref, hp, value):
-        for i in range(4):
-            half, j = i % 2, i // 2
-            ref[4 * hp + i] = value[
-                half * PIECE : (half + 1) * PIECE, j * N : (j + 1) * N].astype(BF)
+        for i in range(8):
+            ref[8 * hp + i] = value[
+                (i % 4) * PART : (i % 4 + 1) * PART, (i // 4) * N : (i // 4 + 1) * N].astype(BF)
 
     def get_pair(ref, hp):
-        v = ref[pl.ds(4 * hp, 4)]
-        return jnp.concatenate([v[:2].reshape(N, N), v[2:].reshape(N, N)], axis=1)
-
-    def increments(k):
-        hp = lax.rem(me // 4 + k, PAIRS)
+        v = ref[pl.ds(8 * hp, 8)]
+        return jnp.concatenate([v[:4].reshape(N, N), v[4:].reshape(N, N)], axis=1)
+
+    def wait_group(group, ref, sem):
+        wait_for(ref.at[pl.ds(SEQ * group, SEQ - 1)], g_rsem.at[2 * (sem - 13) + group])
+
+    def increments(hp):
         wide = dot(weight_ref[...], pick(hp)[: 2 * HEADS])
         sc = (x_ref[:, cols(hp)].astype(F32) * wide).astype(BF)
         sc_ref[hp] = sc
         put_pair(es_ref, hp, dot(b_t, sc))
         send_pair(hp, es_ref, re_ref, 13)
 
-    loop(PAIRS, increments)
-    re_ref[me] = es_ref[me]
+    for group in range(2):
+        loop(4, lambda k: increments(pair_of(group, k + 2)))
+        re_ref[SEQ * group + me] = es_ref[SEQ * group + me]
 
     sum_c1.third()
     stack_ref[0:T] = jnp.concatenate(split3(cum), axis=1).astype(BF)
@@ -277,18 +300,19 @@
 
     wait_for(ce_ref.at[pl.ds(0, SEQ - 1)], rsem.at[12])
     ends = jnp.concatenate(split3(ce_ref[...].reshape(SEQ, N)[:, :HEADS]), axis=1).astype(BF)
-    sel_own = jnp.where(sel_row[:, :N] == head0 + me // 2, 1.0, 0.0).astype(BF)
-    dec_ref[...] = jnp.exp(dot(ends, sel_own))
-    wait_for(re_ref.at[pl.ds(0, SEQ - 1)], rsem.at[13])
-
-    def forward(j, state):
-        sf_ref[j] = state.astype(BF)
-        return dec_ref[pl.ds(j, 1), :] * state + re_ref[j].astype(F32)
-
-    lax.fori_loop(0, SEQ, forward, jnp.zeros((PIECE, N), F32), unroll=4)
-    loop(SEQ - 1, lambda k: send(
-        sf_ref.at[peer(k + 1)], rs_ref.at[me], ssem.at[14], s_rsem.at[me], (peer(k + 1), dq)))
-    rs_ref[me] = sf_ref[me]
+    for group in range(2):
+        sel_own = jnp.where(
+            sel_row[:, :N] == head0 + 8 * group + me // 4, 1.0, 0.0).astype(BF)
+        dec_ref[SEQ * group : SEQ * group + SEQ] = jnp.exp(dot(ends, sel_own))
+
+    def forward(at, state):
+        sf_ref[at] = state.astype(BF)
+        return dec_ref[pl.ds(at, 1), :] * state + re_ref[at].astype(F32)
+
+    for group in range(2):
+        wait_group(group, re_ref, 13)
+        lax.fori_loop(SEQ * group, SEQ * group + SEQ, forward, jnp.zeros((PART, N), F32), unroll=4)
+        send_all(group, sf_ref, rs_ref, 14, s_rsem)
 
     def turn(i):
         at = pl.ds(pl.multiple_of(i * 2 * N, 2 * N), 2 * N)
@@ -297,8 +321,7 @@
     loop(PAIRS, turn)
     acc_ref[...] = jnp.zeros_like(acc_ref)
 
-    def errors(k):
-        hp = lax.rem(me // 4 + PAIRS - k, PAIRS)
+    def errors(hp):
         at = cols(hp)
         wait_pair(hp, rs_ref, s_rsem)
         decay = jnp.exp(cx_ref[hp])
@@ -312,8 +335,9 @@
         send_pair(hp, gs_ref, rg_ref, 15)
         acc_ref[0:8] += jnp.sum((err * err).reshape(T // 8, 8, 2 * N), axis=0)
 
-    loop(PAIRS, errors)
-    rg_ref[me] = gs_ref[me]
+    for group in range(2):
+        loop(4, lambda k: errors(pair_of(group, 4 - k)))
+        rg_ref[SEQ * group + me] = gs_ref[SEQ * group + me]
 
     lane = lax.broadcasted_iota(jnp.int32, (T, HEADS), 1)
     lane1 = lax.broadcasted_iota(jnp.int32, (1, HEADS), 1)
@@ -346,17 +370,16 @@
     db_ref[...] = dot(dsc.T.astype(BF), c_out)
     sum_c.second()
     k_cols = k_ref[...].T[:, :HEADS]
-    wait_for(rg_ref.at[pl.ds(0, SEQ - 1)], rsem.at[15])
-
-    def backward(i, state):
-        j = SEQ - 1 - i
-        sh_ref[j] = state.astype(BF)
-        return dec_ref[pl.ds(j, 1), :] * state + rg_ref[j].astype(F32)
-
-    lax.fori_loop(0, SEQ, backward, jnp.zeros((PIECE, N), F32), unroll=4)
-    loop(SEQ - 1, lambda k: send(
-        sh_ref.at[peer(k + 1)], rh_ref.at[me], ssem.at[16], h_rsem.at[me], (peer(k + 1), dq)))
-    rh_ref[me] = sh_ref[me]
+    def backward(i, state, group):
+        at = SEQ * group + SEQ - 1 - i
+        sh_ref[at] = state.astype(BF)
+        return dec_ref[pl.ds(at, 1), :] * state + rg_ref[at].astype(F32)
+
+    for group in range(2):
+        wait_group(group, rg_ref, 15)
+        lax.fori_loop(0, SEQ, functools.partial(backward, group=group),
+                      jnp.zeros((PART, N), F32), unroll=4)
+        send_all(group, sh_ref, rh_ref, 16, h_rsem)
 
     sum_c.third()
     sum_c.last()
@@ -421,8 +444,7 @@
 
         loop(8, one)
 
-    def grads_of_state(k):
-        hp = lax.rem(me // 4 + PAIRS - k, PAIRS)
+    def grads_of_state(hp):
         wait_pair(hp, rh_ref, h_rsem)
         after = get_pair(rh_ref, hp)
         db_ref[...] += dot_nt(sc_ref[hp], after)
@@ -437,7 +459,8 @@
             acc_ref[9:10, :HEADS] += jnp.where(
                 lane1 == head, jnp.sum(decayed[:, sub], axis=1, keepdims=True), 0.0)
 
-    loop(PAIRS, grads_of_state)
+    for group in range(2):
+        loop(4, lambda k: grads_of_state(pair_of(group, 4 - k)))
 
     left = jnp.exp(cend - cum)
     d_weight = dw_ref[...] * left
@@ -466,7 +489,7 @@
 
     @pl.when(me != 0)
     def _():
-        send(sums_ref, sroot_ref.at[me], ssem.at[21], rsem.at[21], (0, dq))
+        send(sums_ref, sroot_ref.at[me], ssem.at[24], rsem.at[24], (0, dq))
 
     lines_to_planes()
     sum_b.third()
@@ -477,50 +500,53 @@
 
     def terms_b(g):
         part = xt_ref[pl.ds(pl.multiple_of(g * 512, 512), 512), :]
-        wsb_ref[pl.ds(8 * g, 8), 0:PIECE] = dot(part, g_b).astype(BF).reshape(8, PIECE, N)
+        term = dot(part, g_b).astype(BF).reshape(8, PIECE, N)
+        for i in range(2):
+            wsb_ref[i, pl.ds(8 * g, 8)] = term[:, 32 * i : 32 * i + 32]
+
+    def terms_dt(g):
         wide = dot(g_dt, x_ref[:, pl.ds(pl.multiple_of(g * 512, 512), 512)]).astype(BF)
         for i in range(4):
             for j in range(2):
-                wsb_ref[4 * g + i + 16 * j, PIECE : PIECE + 32] = wide[
-                    32 * j : 32 * j + 32, N * i : N * i + N]
+                wsb_ref[2, 4 * g + i + 16 * j] = wide[32 * j : 32 * j + 32, N * i : N * i + N]
+
+    def send_terms(i):
+        to_peers(lambda o: send(
+            wsb_ref.at[i, o], rwb_ref.at[i, me], ssem.at[19], w_rsem.at[i], (o, dq)))
+        rwb_ref[i, me] = wsb_ref[i, me]
 
     loop(4, terms_b)
-    to_peers(lambda o: send(wsb_ref.at[o], rwb_ref.at[me], ssem.at[19], w_rsem.at[me], (o, dq)))
-    rwb_ref[me] = wsb_ref[me]
+    send_terms(0)
+    loop(4, terms_dt)
+    send_terms(1)
+    send_terms(2)
     planes_back()
 
     @pl.when(me == 0)
     def _():
         sroot_ref[0] = sums_ref[...]
-        wait_for(sroot_ref.at[pl.ds(0, SEQ - 1)], rsem.at[21])
+        wait_for(sroot_ref.at[pl.ds(0, SEQ - 1)], rsem.at[24])
         sdp_ref[dq] = jnp.sum(sroot_ref[...], axis=0)
         for k in range(1, DP):
             send(sdp_ref.at[dq], sdp_ref.at[dq], ssem.at[22], rsem.at[22],
                  (me, lax.rem(dq + k, DP)))
 
+    own_parts = [wbc_ref.at[me, pl.ds(32 * i, 32), pl.ds(0, N)] for i in range(2)] + [
+        wdt_ref.at[pl.ds(pl.multiple_of(32 * (me // 16), 32), 32),
+                   pl.ds(pl.multiple_of(N * lax.rem(me, 16), N), N)]]
+
+    def total_of(i):
+        wait_for(rwb_ref.at[i, pl.ds(0, SEQ - 1)], w_rsem.at[i])
+        total = lax.fori_loop(
+            1, SEQ, lambda j, v: v + rwb_ref[i, j].astype(F32), rwb_ref[i, 0].astype(F32), unroll=4)
+        own_parts[i][...] = total.astype(BF)
+        to_peers(lambda o: send(
+            own_parts[i], own_parts[i], ssem.at[20], rsem.at[19 + i], (o, dq)))
+
+    total_of(0)
+    total_of(1)
+    total_of(2)
     lines_back()
-
-    def add(k, so_far):
-        o = offset(1 + k // 16, lax.rem(2 + 3 * (k // 4), 4), lax.rem(2 + 3 * k, 4))
-
-        @pl.when(o != me)
-        def _():
-            wait_for(rwb_ref.at[o], w_rsem.at[o])
-
-        return so_far + rwb_ref[o].astype(F32)
-
-    total = lax.fori_loop(0, SEQ, add, jnp.zeros((PIECE + 32, N), F32)).astype(BF)
-    wbc_ref[me, :, :N] = total[:PIECE]
-    own_b = wbc_ref.at[me, :, pl.ds(0, N)]
-    own_dt = wdt_ref.at[pl.ds(pl.multiple_of(32 * (me // 16), 32), 32),
-                        pl.ds(pl.multiple_of(N * lax.rem(me, 16), N), N)]
-    own_dt[...] = total[PIECE:]
-
-    def last_sends(o):
-        send(own_b, own_b, ssem.at[20], rsem.at[20], (o, dq))
-        send(own_dt, own_dt, ssem.at[24], rsem.at[24], (o, dq))
-
-    to_peers(last_sends)
 
     @pl.when(me == 0)
     def _():
@@ -533,7 +559,7 @@
 
     @pl.when(me != 0)
     def _():
-        wait_for(sums_ref, ssem.at[21])
+        wait_for(sums_ref, ssem.at[24])
         wait_for(sfin_ref, rsem.at[23])
 
     small_ref[...] = sfin_ref[...]
@@ -541,18 +567,21 @@
     for one in (sum_b1, sum_c1, sum_dt, sum_c, sum_b):
         one.sent()
     pieces = pl.ds(0, SEQ - 1)
-    for sem, ref in ((12, ce_ref), (13, es_ref), (14, sf_ref), (15, gs_ref), (16, sh_ref),
-                     (19, wsb_ref), (20, sf_ref)):
-        wait_for(ref.at[pieces], ssem.at[sem])
-    wait_for(wsb_ref.at[pieces, pl.ds(0, 32)], ssem.at[24])
+    both = pl.ds(0, 2 * SEQ - 2)
+    wait_for(ce_ref.at[pieces], ssem.at[12])
+    for sem, ref in ((13, es_ref), (14, sf_ref), (15, gs_ref), (16, sh_ref)):
+        wait_for(ref.at[both], ssem.at[sem])
+    for sem in (19, 20):
+        for i in range(3):
+            wait_for(wsb_ref.at[i, pieces], ssem.at[sem])
+    for i in range(3):
+        wait_for(wsb_ref.at[i, pieces], rsem.at[19 + i])
     for i in range(2):
         wait_for(z1_s.at[pl.ds(0, 3)], ssem.at[17 + i])
         wait_for(z2_s.at[pl.ds(0, 7)], ssem.at[28 + i])
         wait_for(z2_s.at[pl.ds(0, 7)], ssem.at[30 + i])
         wait_for(z1_s.at[pl.ds(0, 3)], ssem.at[32 + i])
         wait_for(z1_s.at[pl.ds(0, 3)], rsem.at[32 + i])
-    wait_for(wbc_ref.at[pieces, :, pl.ds(0, N)], rsem.at[20])
-    wait_for(rwb_ref.at[pieces, pl.ds(0, 32)], rsem.at[24])
 
 
 def widen(wbc_ref, wdt_ref, small_ref, bc_hbm, dt_hbm, loss_ref, *rest):
@@ -595,12 +624,13 @@
         buf(2 * PAIRS, T, T), f32(PAIRS, T, 2 * N), f32(PAIRS, T, 2 * N), buf(PAIRS, T, 2 * N),
         f32(T, T), f32(T, T), f32(T, N), f32(T, N), f32(2 * HEADS, T), f32(T, HEADS), f32(T, HEADS),
         f32(16, 2 * N),
-        f32(SEQ, 1, N), *[buf(SEQ, PIECE, N) for _ in range(8)], f32(SEQ, N),
+        f32(SEQ, 1, N), *[buf(2 * SEQ, PART, N) for _ in range(8)], f32(2 * SEQ, N),
         *[buf(4, 8, 32, N) for _ in range(4)], *[buf(8, 32, N) for _ in range(4)],
-        buf(SEQ, PIECE + 32, N), buf(SEQ, PIECE + 32, N),
+        buf(3, SEQ, 32, N), buf(3, SEQ, 32, N),
         f32(8, 128), f32(SEQ, 8, 128), f32(DP, 8, 128), f32(8, 128),
         pltpu.SemaphoreType.DMA((34,)), pltpu.SemaphoreType.DMA((34,)),
-        *[pltpu.SemaphoreType.DMA((SEQ,)) for _ in range(3)],
+        pltpu.SemaphoreType.DMA((6,)), pltpu.SemaphoreType.DMA((PAIRS,)),
+        pltpu.SemaphoreType.DMA((PAIRS,)), pltpu.SemaphoreType.DMA((3,)),
         pltpu.SemaphoreType.DMA((4,)), pltpu.SemaphoreType.REGULAR((2,)),
     ]
     state_grad, step_grad, small = pl.pallas_call(

time: 92.4 us -> 86.2 us (0.933)
  Pallas kernels: 90.5 us -> 83.9 us
    pallas_call x1, Pallas kernels: 88.4 us -> 81.8 us  [shards(): pl.pallas_call(kernel, out_shape=(jax.ShapeDtypeStruct((SEQ, PIECE, 2 * N...]
where the time goes in v4:
time: 86.2 us; the launch traced here: 85.3 us
  Pallas kernels  83.9 us (97%)
    pallas_call x1, Pallas kernels, shards(): pl.pallas_call(kernel, out_shape=(jax.ShapeDtypeStruct((SEQ, PIECE, 2 * N...  81.8 us
    pallas_call x1, Pallas kernels, shards(): pl.pallas_call(widen, out_shape=(jax.ShapeDtypeStruct((WIDTH, 2 * N), F32...  2.09 us

profile of v4, /device:TPU:0, one launch (start us, length us, event | category | flops | bytes accessed | tf_op | source)
XLA Modules:
  0.0 85.3 jit_solution(13382513398044007807)
XLA Ops:
  0.6 0.7 pad_maximum_fusion.heads_ref
  1.3 81.8 %shard_map.118 = (bf16[32,64,256]{2,1,0:T(8,128)(2,1)S(1)}, bf16[64,2048]{1,0:T(8,128)(2,1)S(1)}, f32[8,128]{1,0:T(8,128)S(1)}) custom-call(bf16[256,2048]{1,0:T(8,128)(2,1)} %x_hbm.1, bf16[256,2048]{1,0:T(8,128)(2,1)} %tgt_hbm.1, bf16[8192,256]{1,0:T(8,128)(2,1)} %sp_ref.1, bf16[64,8192]{1,0:T(8,128)(2,1)} %bitcast.9, f32[3,64]{1,0:T(4,128)S(1)} %pad_maximum_fusion.heads_ref), custom_call_target="tpu_custom_call" | custom-call | tf_op jit(solution)/shard_map/pallas_call | solution.py:636
  83.2 2.1 %shard_map.119 = (f32[2048,256]{1,0:T(8,128)}, f32[64,2048]{1,0:T(8,128)}, f32[1,1]{1,0:T(1,128)}, f32[1,64]{1,0:T(1,128)}, f32[1,64]{1,0:T(1,128)}, /*index=5*/f32[1,64]{1,0:T(1,128)}) custom-call(bf16[32,64,256]{2,1,0:T(8,128)(2,1)S(1)} %get-tuple-element.15.wbc_ref, bf16[64,2048]{1,0:T(8,128)(2,1)S(1)} %get-tuple-element.16.wdt_ref, ...), custom_call_target="tpu_custom_call" | custom-call | tf_op jit(solution)/shard_map/pallas_call | solution.py:651

commit v5 on v4

--- a/solution.py
+++ b/solution.py
@@ -75,7 +75,7 @@
     sm_ref, dsc_ref, dc_ref, db_ref, k_ref, a_ref, dw_ref, acc_ref,
     ce_ref, es_ref, re_ref, sf_ref, rs_ref, gs_ref, rg_ref, sh_ref, rh_ref, dec_ref,
     z1_s, z1_r, x1_s, x1_r, z2_s, z2_r, x2_s, x2_r, wsb_ref, rwb_ref, sums_ref, sroot_ref, sdp_ref, sfin_ref,
-    ssem, rsem, g_rsem, s_rsem, h_rsem, w_rsem, lsem, go,
+    ssem, rsem, g_rsem, s_rsem, w_rsem, lsem, go,
 ):
     me, dq = lax.axis_index("seq"), lax.axis_index("dp")
     head0 = dq * (HEADS // DP)
@@ -178,9 +178,7 @@
     sum_dt.third()
     sum_b1.third()
     sum_dt.last()
-    sum_b1.last()
-
-    b_in = m0_f[...].reshape(T, N)
+
     pre = unpack_rows(d1_f) + heads_ref[1:2]
     dt = jnp.maximum(pre, 0.0) + jnp.log1p(jnp.exp(-jnp.abs(pre)))
     rate = jnp.exp(heads_ref[0:1])
@@ -190,11 +188,13 @@
     tri = jnp.where(row_i >= col_i, 1.0, 0.0).astype(BF)
     cum = tri_sum(tri, log_rate)
     cend = cum[T - 1 : T]
-    b_t = b_in.astype(F32).T.astype(BF)
     weight = dt * jnp.exp(cend - cum)
     high = weight.astype(BF).astype(F32)
     weight_ref[...] = jnp.concatenate([high, weight - high], axis=1).astype(BF)
     ce_ref[me] = jnp.concatenate([cend, cend], axis=1)
+    sum_b1.last()
+    b_in = m0_f[...].reshape(T, N)
+    b_t = b_in.astype(F32).T.astype(BF)
     pl.semaphore_wait(go.at[1], 1)
     loop(SEQ - 1, lambda k: send(
         ce_ref.at[me], ce_ref.at[me], ssem.at[12], rsem.at[12], (peer(k + 1), dq)))
@@ -237,11 +237,11 @@
         def _():
             wait_for(ref.at[pl.ds(8 * hp, 8)], sems.at[hp])
 
-    def send_all(group, src, dst, sem, sems):
+    def send_all(group, src, dst, sem, sems, slot=None):
         def one(k):
             o = peer(k + 1)
             send(src.at[SEQ * group + o], dst.at[SEQ * group + me],
-                 ssem.at[sem], sems.at[(SEQ * group + me) // 8], (o, dq))
+                 ssem.at[sem], sems.at[(SEQ * group + me) // 8 if slot is None else slot], (o, dq))
 
         loop(SEQ - 1, one)
         dst[SEQ * group + me] = src[SEQ * group + me]
@@ -258,16 +258,19 @@
     def wait_group(group, ref, sem):
         wait_for(ref.at[pl.ds(SEQ * group, SEQ - 1)], g_rsem.at[2 * (sem - 13) + group])
 
-    def increments(hp):
-        wide = dot(weight_ref[...], pick(hp)[: 2 * HEADS])
-        sc = (x_ref[:, cols(hp)].astype(F32) * wide).astype(BF)
-        sc_ref[hp] = sc
-        put_pair(es_ref, hp, dot(b_t, sc))
-        send_pair(hp, es_ref, re_ref, 13)
-
+    wide_row = lax.rem(lax.broadcasted_iota(jnp.int32, (2 * HEADS, 8 * N), 0), HEADS)
+    wide_col = lax.broadcasted_iota(jnp.int32, (2 * HEADS, 8 * N), 1) // N
     for group in range(2):
-        loop(4, lambda k: increments(pair_of(group, k + 2)))
-        re_ref[SEQ * group + me] = es_ref[SEQ * group + me]
+        sel = jnp.where(wide_row == head0 + 8 * group + wide_col, 1.0, 0.0).astype(BF)
+        wide = dot(weight_ref[...], sel)
+        at = slice(8 * N * group, 8 * N * (group + 1))
+        sc = (x_ref[:, at].astype(F32) * wide).astype(BF)
+        sc_ref[group] = sc
+        term = dot(b_t, sc).astype(BF)
+        for i in range(SEQ):
+            es_ref[SEQ * group + i] = term[
+                (i % 4) * PART : (i % 4 + 1) * PART, (i // 4) * N : (i // 4 + 1) * N]
+        send_all(group, es_ref, re_ref, 13, g_rsem, group)
 
     sum_c1.third()
     stack_ref[0:T] = jnp.concatenate(split3(cum), axis=1).astype(BF)
@@ -311,7 +314,7 @@
 
     for group in range(2):
         wait_group(group, re_ref, 13)
-        lax.fori_loop(SEQ * group, SEQ * group + SEQ, forward, jnp.zeros((PART, N), F32), unroll=4)
+        lax.fori_loop(SEQ * group, SEQ * group + SEQ, forward, jnp.zeros((PART, N), F32), unroll=8)
         send_all(group, sf_ref, rs_ref, 14, s_rsem)
 
     def turn(i):
@@ -332,12 +335,11 @@
         de = (err * decay).astype(BF)
         de_ref[hp] = de
         put_pair(gs_ref, hp, dot(c_t, de))
-        send_pair(hp, gs_ref, rg_ref, 15)
         acc_ref[0:8] += jnp.sum((err * err).reshape(T // 8, 8, 2 * N), axis=0)
 
     for group in range(2):
         loop(4, lambda k: errors(pair_of(group, 4 - k)))
-        rg_ref[SEQ * group + me] = gs_ref[SEQ * group + me]
+        send_all(group, gs_ref, rg_ref, 15, g_rsem, 4 + group)
 
     lane = lax.broadcasted_iota(jnp.int32, (T, HEADS), 1)
     lane1 = lax.broadcasted_iota(jnp.int32, (1, HEADS), 1)
@@ -378,8 +380,8 @@
     for group in range(2):
         wait_group(group, rg_ref, 15)
         lax.fori_loop(0, SEQ, functools.partial(backward, group=group),
-                      jnp.zeros((PART, N), F32), unroll=4)
-        send_all(group, sh_ref, rh_ref, 16, h_rsem)
+                      jnp.zeros((PART, N), F32), unroll=8)
+        send_all(group, sh_ref, rh_ref, 16, g_rsem, 6 + group)
 
     sum_c.third()
     sum_c.last()
@@ -444,28 +446,29 @@
 
         loop(8, one)
 
-    def grads_of_state(hp):
-        wait_pair(hp, rh_ref, h_rsem)
-        after = get_pair(rh_ref, hp)
-        db_ref[...] += dot_nt(sc_ref[hp], after)
-        weighed = dot(b_in, after) * x_ref[:, cols(hp)].astype(F32)
-        decayed = jnp.sum(
-            after.astype(F32) * get_pair(rs_ref, hp).astype(F32), axis=0, keepdims=True)
-        for j in range(2):
-            head = head0 + 2 * hp + j
-            sub = slice(j * N, (j + 1) * N)
-            dw_ref[...] += jnp.where(
-                lane == head, jnp.sum(weighed[:, sub], axis=1, keepdims=True), 0.0)
-            acc_ref[9:10, :HEADS] += jnp.where(
-                lane1 == head, jnp.sum(decayed[:, sub], axis=1, keepdims=True), 0.0)
-
+    sum_row = lax.broadcasted_iota(jnp.int32, (8 * N, HEADS), 0) // N
+    sum_col = lax.broadcasted_iota(jnp.int32, (8 * N, HEADS), 1)
     for group in range(2):
-        loop(4, lambda k: grads_of_state(pair_of(group, 4 - k)))
+        to_head = jnp.where(sum_col == head0 + 8 * group + sum_row, 1.0, 0.0).astype(BF)
+
+        def by_head(v):
+            high = v.astype(BF)
+            return dot(high, to_head) + dot((v - high.astype(F32)).astype(BF), to_head)
+
+        wait_group(group, rh_ref, 16)
+        pairs = range(4 * group, 4 * group + 4)
+        after = jnp.concatenate([get_pair(rh_ref, hp) for hp in pairs], axis=1)
+        before = jnp.concatenate([get_pair(rs_ref, hp) for hp in pairs], axis=1)
+        at = slice(8 * N * group, 8 * N * (group + 1))
+        db_ref[...] += dot_nt(sc_ref[group], after)
+        dw_ref[...] += by_head(dot(b_in, after) * x_ref[:, at].astype(F32))
+        decayed = after.astype(F32) * before.astype(F32)
+        acc_ref[16:24, :HEADS] += by_head(jnp.sum(decayed.reshape(16, 8, 8 * N), axis=0))
 
     left = jnp.exp(cend - cum)
     d_weight = dw_ref[...] * left
     d_gap = d_weight * dt
-    d_end = jnp.sum(d_gap, axis=0, keepdims=True) + jnp.exp(cend) * acc_ref[9:10, :HEADS]
+    d_end = jnp.sum(d_gap, axis=0, keepdims=True) + jnp.exp(cend) * jnp.sum(acc_ref[16:24, :HEADS], axis=0, keepdims=True)
     d_cum = a_ref[...] - k_cols * dt - d_gap
     tri_up = jnp.where(row_i <= col_i, 1.0, 0.0).astype(BF)
     d_log = tri_sum(tri_up, d_cum) + d_end
@@ -498,12 +501,6 @@
     g_b = m3_f[:, 0:128].reshape(T, N)
     g_dt = unpack_rows(m3_f.at[:, pl.ds(128, 64)]).astype(F32).T.astype(BF)
 
-    def terms_b(g):
-        part = xt_ref[pl.ds(pl.multiple_of(g * 512, 512), 512), :]
-        term = dot(part, g_b).astype(BF).reshape(8, PIECE, N)
-        for i in range(2):
-            wsb_ref[i, pl.ds(8 * g, 8)] = term[:, 32 * i : 32 * i + 32]
-
     def terms_dt(g):
         wide = dot(g_dt, x_ref[:, pl.ds(pl.multiple_of(g * 512, 512), 512)]).astype(BF)
         for i in range(4):
@@ -515,7 +512,9 @@
             wsb_ref.at[i, o], rwb_ref.at[i, me], ssem.at[19], w_rsem.at[i], (o, dq)))
         rwb_ref[i, me] = wsb_ref[i, me]
 
-    loop(4, terms_b)
+    term = dot(xt_ref[...], g_b).astype(BF).reshape(SEQ, PIECE, N)
+    for i in range(2):
+        wsb_ref[i] = term[:, 32 * i : 32 * i + 32]
     send_terms(0)
     loop(4, terms_dt)
     send_terms(1)
@@ -584,20 +583,24 @@
         wait_for(z1_s.at[pl.ds(0, 3)], rsem.at[32 + i])
 
 
-def widen(wbc_ref, wdt_ref, small_ref, bc_hbm, dt_hbm, loss_ref, *rest):
-    sums, (bc_ref, dt_ref, sem) = rest[:3], rest[3:]
+def widen(wbc_ref, wdt_ref, small_ref, bc_hbm, dt_hbm, *rest):
+    outs, (bc_ref, dt_ref, loss_ref, heads_ref, sem) = rest[:4], rest[4:]
     copies = []
+
+    def put(src, dst):
+        copies.append(pltpu.make_async_copy(src, dst, sem.at[len(copies)]))
+        copies[-1].start()
+
+    loss_ref[...] = small_ref[0:1, 0:1]
+    put(loss_ref, outs[0])
+    for i in range(3):
+        heads_ref[i] = small_ref[i + 1 : i + 2, :HEADS]
+        put(heads_ref.at[i], outs[i + 1])
+    dt_ref[...] = wdt_ref[...].astype(F32)
+    put(dt_ref, dt_hbm)
     for i in range(4):
         bc_ref[i] = wbc_ref[8 * i : 8 * i + 8].astype(F32).reshape(512, 2 * N)
-        copies.append(pltpu.make_async_copy(
-            bc_ref.at[i], bc_hbm.at[pl.ds(512 * i, 512)], sem.at[i]))
-        copies[-1].start()
-    dt_ref[...] = wdt_ref[...].astype(F32)
-    copies.append(pltpu.make_async_copy(dt_ref, dt_hbm, sem.at[4]))
-    copies[-1].start()
-    loss_ref[...] = small_ref[0:1, 0:1]
-    for i, ref in enumerate(sums):
-        ref[...] = small_ref[i + 1 : i + 2, :HEADS]
+        put(bc_ref.at[i], bc_hbm.at[pl.ds(512 * i, 512)])
     for one in copies:
         one.wait()
 
@@ -620,17 +623,16 @@
         buf(T, WIDTH), buf(T, WIDTH), buf(WIDTH, 2 * N), buf(HEADS, WIDTH), buf(WIDTH, T),
         *dp_bufs(128, buf), *dp_bufs(128, buf), *dp_bufs(64, f32), *dp_bufs(128, buf), *dp_bufs(192, buf),
         buf(T, 2 * HEADS), buf(2 * T, 3 * HEADS), buf(16, 3 * HEADS), f32(2 * HEADS, T),
-        f32(PAIRS, T, 2 * N), f32(PAIRS, 8, 2 * N), buf(PAIRS, T, 2 * N),
+        f32(PAIRS, T, 2 * N), f32(PAIRS, 8, 2 * N), buf(2, T, 8 * N),
         buf(2 * PAIRS, T, T), f32(PAIRS, T, 2 * N), f32(PAIRS, T, 2 * N), buf(PAIRS, T, 2 * N),
         f32(T, T), f32(T, T), f32(T, N), f32(T, N), f32(2 * HEADS, T), f32(T, HEADS), f32(T, HEADS),
-        f32(16, 2 * N),
+        f32(24, 2 * N),
         f32(SEQ, 1, N), *[buf(2 * SEQ, PART, N) for _ in range(8)], f32(2 * SEQ, N),
         *[buf(4, 8, 32, N) for _ in range(4)], *[buf(8, 32, N) for _ in range(4)],
         buf(3, SEQ, 32, N), buf(3, SEQ, 32, N),
         f32(8, 128), f32(SEQ, 8, 128), f32(DP, 8, 128), f32(8, 128),
         pltpu.SemaphoreType.DMA((34,)), pltpu.SemaphoreType.DMA((34,)),
-        pltpu.SemaphoreType.DMA((6,)), pltpu.SemaphoreType.DMA((PAIRS,)),
-        pltpu.SemaphoreType.DMA((PAIRS,)), pltpu.SemaphoreType.DMA((3,)),
+        pltpu.SemaphoreType.DMA((8,)), pltpu.SemaphoreType.DMA((PAIRS,)), pltpu.SemaphoreType.DMA((3,)),
         pltpu.SemaphoreType.DMA((4,)), pltpu.SemaphoreType.REGULAR((2,)),
     ]
     state_grad, step_grad, small = pl.pallas_call(
@@ -656,8 +658,9 @@
             jax.ShapeDtypeStruct((1, 1), F32), heads, heads, heads,
         ),
         in_specs=[vmem] * 3,
-        out_specs=(hbm, hbm, vmem, vmem, vmem, vmem),
-        scratch_shapes=[f32(4, 512, 2 * N), f32(HEADS, WIDTH), pltpu.SemaphoreType.DMA((5,))],
+        out_specs=(hbm,) * 6,
+        scratch_shapes=[f32(4, 512, 2 * N), f32(HEADS, WIDTH), f32(1, 1), f32(3, 1, HEADS),
+                        pltpu.SemaphoreType.DMA((9,))],
         compiler_params=pltpu.CompilerParams(vmem_limit_bytes=16 * 1024 * 1024),
     )(state_grad, step_grad, small)
     return (loss[0, 0], state_grad, step_grad.T, *(v[0] for v in sums))

time: 86.2 us -> 82.9 us (0.962)
  Pallas kernels: 83.9 us -> 80.6 us
    pallas_call x1, Pallas kernels: 81.8 us -> 79 us  [shards(): pl.pallas_call(kernel, out_shape=(jax.ShapeDtypeStruct((SEQ, PIECE, 2 * N...]
where the time goes in v5:
time: 82.9 us; the launch traced here: 82 us
  Pallas kernels  80.6 us (97%)
    pallas_call x1, Pallas kernels, shards(): pl.pallas_call(kernel, out_shape=(jax.ShapeDtypeStruct((SEQ, PIECE, 2 * N...  79 us

profile of v5, /device:TPU:0, one launch (start us, length us, event | category | flops | bytes accessed | tf_op | source)
XLA Modules:
  0.0 82.0 jit_solution(18236959959661538036)
XLA Ops:
  0.6 0.7 pad_maximum_fusion.heads_ref
  1.3 79.0 %shard_map.118 = (bf16[32,64,256]{2,1,0:T(8,128)(2,1)S(1)}, bf16[64,2048]{1,0:T(8,128)(2,1)S(1)}, f32[8,128]{1,0:T(8,128)S(1)}) custom-call(bf16[256,2048]{1,0:T(8,128)(2,1)} %x_hbm.1, bf16[256,2048]{1,0:T(8,128)(2,1)} %tgt_hbm.1, bf16[8192,256]{1,0:T(8,128)(2,1)} %sp_ref.1, bf16[64,8192]{1,0:T(8,128)(2,1)} %bitcast.9, f32[3,64]{1,0:T(4,128)S(1)} %pad_maximum_fusion.heads_ref), custom_call_target="tpu_custom_call" | custom-call | tf_op jit(solution)/shard_map/pallas_call | solution.py:638
  80.4 1.6 %shard_map.119 = (f32[2048,256]{1,0:T(8,128)}, f32[64,2048]{1,0:T(8,128)}, f32[1,1]{1,0:T(1,128)}, f32[1,64]{1,0:T(1,128)}, f32[1,64]{1,0:T(1,128)}, /*index=5*/f32[1,64]{1,0:T(1,128)}) custom-call(bf16[32,64,256]{2,1,0:T(8,128)(2,1)S(1)} %get-tuple-element.15.wbc_ref, bf16[64,2048]{1,0:T(8,128)(2,1)S(1)} %get-tuple-element.16.wdt_ref, ...), custom_call_target="tpu_custom_call" | custom-call | tf_op jit(solution)/shard_map/pallas_call | solution.py:653

commit v6 on v5

--- a/solution.py
+++ b/solution.py
@@ -519,7 +519,6 @@
     loop(4, terms_dt)
     send_terms(1)
     send_terms(2)
-    planes_back()
 
     @pl.when(me == 0)
     def _():
@@ -537,12 +536,13 @@
     def total_of(i):
         wait_for(rwb_ref.at[i, pl.ds(0, SEQ - 1)], w_rsem.at[i])
         total = lax.fori_loop(
-            1, SEQ, lambda j, v: v + rwb_ref[i, j].astype(F32), rwb_ref[i, 0].astype(F32), unroll=4)
+            1, SEQ, lambda j, v: v + rwb_ref[i, j].astype(F32), rwb_ref[i, 0].astype(F32), unroll=31)
         own_parts[i][...] = total.astype(BF)
         to_peers(lambda o: send(
             own_parts[i], own_parts[i], ssem.at[20], rsem.at[19 + i], (o, dq)))
 
     total_of(0)
+    planes_back()
     total_of(1)
     total_of(2)
     lines_back()

time: 82.9 us -> 82.1 us (level)
  no operation moved by 1% of the time
where the time goes in v6:
time: 82.1 us; the launch traced here: 81.9 us
  Pallas kernels  80.6 us (98%)
    pallas_call x1, Pallas kernels, shards(): pl.pallas_call(kernel, out_shape=(jax.ShapeDtypeStruct((SEQ, PIECE, 2 * N...  79 us

profile of v6, /device:TPU:0, one launch (start us, length us, event | category | flops | bytes accessed | tf_op | source)
XLA Modules:
  0.0 81.9 jit_solution(10848372917184038730)
XLA Ops:
  0.6 0.7 pad_maximum_fusion.heads_ref
  1.3 79.0 %shard_map.118 = (bf16[32,64,256]{2,1,0:T(8,128)(2,1)S(1)}, bf16[64,2048]{1,0:T(8,128)(2,1)S(1)}, f32[8,128]{1,0:T(8,128)S(1)}) custom-call(bf16[256,2048]{1,0:T(8,128)(2,1)} %x_hbm.1, bf16[256,2048]{1,0:T(8,128)(2,1)} %tgt_hbm.1, bf16[8192,256]{1,0:T(8,128)(2,1)} %sp_ref.1, bf16[64,8192]{1,0:T(8,128)(2,1)} %bitcast.9, f32[3,64]{1,0:T(4,128)S(1)} %pad_maximum_fusion.heads_ref), custom_call_target="tpu_custom_call" | custom-call | tf_op jit(solution)/shard_map/pallas_call | solution.py:638
  80.3 1.6 %shard_map.119 = (f32[2048,256]{1,0:T(8,128)}, f32[64,2048]{1,0:T(8,128)}, f32[1,1]{1,0:T(1,128)}, f32[1,64]{1,0:T(1,128)}, f32[1,64]{1,0:T(1,128)}, /*index=5*/f32[1,64]{1,0:T(1,128)}) custom-call(bf16[32,64,256]{2,1,0:T(8,128)(2,1)S(1)} %get-tuple-element.15.wbc_ref, bf16[64,2048]{1,0:T(8,128)(2,1)S(1)} %get-tuple-element.16.wdt_ref, ...), custom_call_target="tpu_custom_call" | custom-call | tf_op jit(solution)/shard_map/pallas_call | solution.py:653

commit v7 on v6

--- a/solution.py
+++ b/solution.py
@@ -122,10 +122,11 @@
 
     class DpSum:
         def __init__(self, sem, tmp, sa, ra, sb, rb, f):
+            self.slot = 1 if sem == 25 else sem
             self.sem, self.tmp, self.sa, self.ra, self.sb, self.rb, self.f = sem, tmp, sa, ra, sb, rb, f
 
         def send(self, src, dst, step, member):
-            send(src, dst, ssem.at[self.sem + step], rsem.at[self.sem + step], (me, member))
+            send(src, dst, ssem.at[self.slot], rsem.at[self.sem + step], (me, member))
 
         def first(self):
             self.sa[...] = self.tmp[1 - core].astype(self.sa.dtype)
@@ -148,7 +149,7 @@
 
         def sent(self):
             for step, ref in enumerate((self.sa, self.sb, self.f.at[0])):
-                wait_for(ref, ssem.at[self.sem + step])
+                wait_for(ref, ssem.at[self.slot])
 
     sum_b1 = DpSum(0, m0_tmp, m0_sa, m0_ra, m0_sb, m0_rb, m0_f)
     sum_c1 = DpSum(25, m1_tmp, m1_sa, m1_ra, m1_sb, m1_rb, m1_f)
@@ -398,7 +399,7 @@
         to = lax.rem(my_z + k, 4)
         send(z1_s.at[to], z1_r.at[my_z], ssem.at[17], rsem.at[17], (offset(0, 0, k), dq))
         to = lax.rem(my_x + k, 4)
-        send(x1_s.at[to], x1_r.at[my_x], ssem.at[18], rsem.at[18], (offset(0, k, 0), dq))
+        send(x1_s.at[to], x1_r.at[my_x], ssem.at[17], rsem.at[18], (offset(0, k, 0), dq))
     z1_r[my_z] = z1_s[my_z]
     x1_r[my_x] = x1_s[my_x]
     planes = [(dy, d) for dy in (1, 0) for d in (2, 1, 3, 0)][:7]
@@ -414,9 +415,9 @@
         at_z, at_x = on_plane(0, my_x, 0), on_plane(0, my_z, 0)
         for dy, d in planes:
             send(z2_s.at[on_plane(dy, my_x, d)], z2_r.at[at_z],
-                 ssem.at[28], rsem.at[28], (offset(dy, d, 0), dq))
+                 ssem.at[2], rsem.at[28], (offset(dy, d, 0), dq))
             send(x2_s.at[on_plane(dy, my_z, d)], x2_r.at[at_x],
-                 ssem.at[29], rsem.at[29], (offset(dy, 0, d), dq))
+                 ssem.at[2], rsem.at[29], (offset(dy, 0, d), dq))
         z2_r[at_z] = z2_s[at_z]
         x2_r[at_x] = x2_s[at_x]
 
@@ -429,20 +430,20 @@
         wbc_ref[me, 0:32, N:] = sum(z2_r[i].astype(F32) for i in range(8)).astype(BF)
         wbc_ref[me, 32:64, N:] = sum(x2_r[i].astype(F32) for i in range(8)).astype(BF)
         for dy, d in planes:
-            send(half_of(me, 0), half_of(me, 0), ssem.at[30], rsem.at[30], (offset(dy, d, 0), dq))
-            send(half_of(me, 1), half_of(me, 1), ssem.at[31], rsem.at[31], (offset(dy, 0, d), dq))
+            send(half_of(me, 0), half_of(me, 0), ssem.at[4], rsem.at[13], (offset(dy, d, 0), dq))
+            send(half_of(me, 1), half_of(me, 1), ssem.at[4], rsem.at[14], (offset(dy, 0, d), dq))
 
     def lines_back():
-        wait_for(wbc_ref.at[pl.ds(0, 7), pl.ds(0, 32), pl.ds(N, N)], rsem.at[30])
-        wait_for(wbc_ref.at[pl.ds(0, 7), pl.ds(0, 32), pl.ds(N, N)], rsem.at[31])
+        wait_for(wbc_ref.at[pl.ds(0, 7), pl.ds(0, 32), pl.ds(N, N)], rsem.at[13])
+        wait_for(wbc_ref.at[pl.ds(0, 7), pl.ds(0, 32), pl.ds(N, N)], rsem.at[14])
 
         def one(i):
             y, other = i // 4, lax.rem(i, 4)
             for k in range(1, 4):
                 piece = half_of(16 * y + 4 * other + my_z, 0)
-                send(piece, piece, ssem.at[32], rsem.at[32], (offset(0, 0, k), dq))
+                send(piece, piece, ssem.at[5], rsem.at[15], (offset(0, 0, k), dq))
                 piece = half_of(16 * y + 4 * my_x + other, 1)
-                send(piece, piece, ssem.at[33], rsem.at[33], (offset(0, k, 0), dq))
+                send(piece, piece, ssem.at[5], rsem.at[16], (offset(0, k, 0), dq))
 
         loop(8, one)
 
@@ -492,7 +493,7 @@
 
     @pl.when(me != 0)
     def _():
-        send(sums_ref, sroot_ref.at[me], ssem.at[24], rsem.at[24], (0, dq))
+        send(sums_ref, sroot_ref.at[me], ssem.at[7], rsem.at[24], (0, dq))
 
     lines_to_planes()
     sum_b.third()
@@ -526,7 +527,7 @@
         wait_for(sroot_ref.at[pl.ds(0, SEQ - 1)], rsem.at[24])
         sdp_ref[dq] = jnp.sum(sroot_ref[...], axis=0)
         for k in range(1, DP):
-            send(sdp_ref.at[dq], sdp_ref.at[dq], ssem.at[22], rsem.at[22],
+            send(sdp_ref.at[dq], sdp_ref.at[dq], ssem.at[10], rsem.at[22],
                  (me, lax.rem(dq + k, DP)))
 
     own_parts = [wbc_ref.at[me, pl.ds(32 * i, 32), pl.ds(0, N)] for i in range(2)] + [
@@ -552,13 +553,13 @@
         wait_for(sdp_ref.at[pl.ds(0, DP - 1)], rsem.at[22])
         sfin_ref[...] = jnp.sum(sdp_ref[...], axis=0)
         loop(SEQ - 1, lambda k: send(
-            sfin_ref, sfin_ref, ssem.at[23], rsem.at[23], (peer(k + 1), dq)))
-        wait_for(sdp_ref.at[pl.ds(0, DP - 1)], ssem.at[22])
-        wait_for(sroot_ref.at[pl.ds(0, SEQ - 1)], ssem.at[23])
+            sfin_ref, sfin_ref, ssem.at[8], rsem.at[23], (peer(k + 1), dq)))
+        wait_for(sdp_ref.at[pl.ds(0, DP - 1)], ssem.at[10])
+        wait_for(sroot_ref.at[pl.ds(0, SEQ - 1)], ssem.at[8])
 
     @pl.when(me != 0)
     def _():
-        wait_for(sums_ref, ssem.at[24])
+        wait_for(sums_ref, ssem.at[7])
         wait_for(sfin_ref, rsem.at[23])
 
     small_ref[...] = sfin_ref[...]
@@ -576,11 +577,11 @@
     for i in range(3):
         wait_for(wsb_ref.at[i, pieces], rsem.at[19 + i])
     for i in range(2):
-        wait_for(z1_s.at[pl.ds(0, 3)], ssem.at[17 + i])
-        wait_for(z2_s.at[pl.ds(0, 7)], ssem.at[28 + i])
-        wait_for(z2_s.at[pl.ds(0, 7)], ssem.at[30 + i])
-        wait_for(z1_s.at[pl.ds(0, 3)], ssem.at[32 + i])
-        wait_for(z1_s.at[pl.ds(0, 3)], rsem.at[32 + i])
+        wait_for(z1_s.at[pl.ds(0, 3)], ssem.at[17])
+        wait_for(z2_s.at[pl.ds(0, 7)], ssem.at[2])
+        wait_for(z2_s.at[pl.ds(0, 7)], ssem.at[4])
+        wait_for(z1_s.at[pl.ds(0, 3)], ssem.at[5])
+        wait_for(z1_s.at[pl.ds(0, 3)], rsem.at[15 + i])
 
 
 def widen(wbc_ref, wdt_ref, small_ref, bc_hbm, dt_hbm, *rest):
@@ -631,7 +632,7 @@
         *[buf(4, 8, 32, N) for _ in range(4)], *[buf(8, 32, N) for _ in range(4)],
         buf(3, SEQ, 32, N), buf(3, SEQ, 32, N),
         f32(8, 128), f32(SEQ, 8, 128), f32(DP, 8, 128), f32(8, 128),
-        pltpu.SemaphoreType.DMA((34,)), pltpu.SemaphoreType.DMA((34,)),
+        pltpu.SemaphoreType.DMA((21,)), pltpu.SemaphoreType.DMA((30,)),
         pltpu.SemaphoreType.DMA((8,)), pltpu.SemaphoreType.DMA((PAIRS,)), pltpu.SemaphoreType.DMA((3,)),
         pltpu.SemaphoreType.DMA((4,)), pltpu.SemaphoreType.REGULAR((2,)),
     ]

time: 82.1 us -> 82 us (level)
  no operation moved by 1% of the time
where the time goes in v7:
time: 82 us; the launch traced here: 81.8 us
  Pallas kernels  80.4 us (98%)
    pallas_call x1, Pallas kernels, shards(): pl.pallas_call(kernel, out_shape=(jax.ShapeDtypeStruct((SEQ, PIECE, 2 * N...  78.8 us

profile of v7, /device:TPU:0, one launch (start us, length us, event | category | flops | bytes accessed | tf_op | source)
XLA Modules:
  0.0 81.8 jit_solution(17049458711492630748)
XLA Ops:
  0.6 0.7 pad_maximum_fusion.heads_ref
  1.3 78.8 %shard_map.118 = (bf16[32,64,256]{2,1,0:T(8,128)(2,1)S(1)}, bf16[64,2048]{1,0:T(8,128)(2,1)S(1)}, f32[8,128]{1,0:T(8,128)S(1)}) custom-call(bf16[256,2048]{1,0:T(8,128)(2,1)} %x_hbm.1, bf16[256,2048]{1,0:T(8,128)(2,1)} %tgt_hbm.1, bf16[8192,256]{1,0:T(8,128)(2,1)} %sp_ref.1, bf16[64,8192]{1,0:T(8,128)(2,1)} %bitcast.9, f32[3,64]{1,0:T(4,128)S(1)} %pad_maximum_fusion.heads_ref), custom_call_target="tpu_custom_call" | custom-call | tf_op jit(solution)/shard_map/pallas_call | solution.py:639
  80.2 1.6 %shard_map.119 = (f32[2048,256]{1,0:T(8,128)}, f32[64,2048]{1,0:T(8,128)}, f32[1,1]{1,0:T(1,128)}, f32[1,64]{1,0:T(1,128)}, f32[1,64]{1,0:T(1,128)}, /*index=5*/f32[1,64]{1,0:T(1,128)}) custom-call(bf16[32,64,256]{2,1,0:T(8,128)(2,1)S(1)} %get-tuple-element.15.wbc_ref, bf16[64,2048]{1,0:T(8,128)(2,1)S(1)} %get-tuple-element.16.wdt_ref, ...), custom_call_target="tpu_custom_call" | custom-call | tf_op jit(solution)/shard_map/pallas_call | solution.py:654
